TPU v7x, 128 devices: a whole 4x4x4 slice. The times are simulated.
128 devices in a mesh: lat: 8 (over x, core), lon: 16 (over z, y).
Axes of the slice: x: 4, y: 4, z: 4, core: 2. Of those that a mesh axis runs over, the one named last changes fastest.
Arguments:
- spectra: bfloat16 [65536, 616], P(('lat', 'lon')), may hold values from -6 to 6
- owner: int32 [65536, 1], P(('lat', 'lon')), may hold values from 0 to 127; in each aligned block of 512 rows (0 to 511, 512 to 1023, ...) at most 8 rows name the same one
- cell: int32 [65536], P(('lat', 'lon')), may hold values from 0 to 2047
- w_in: bfloat16 [616, 512], replicated, may hold values from -0.25 to 0.25
- w_out: bfloat16 [512, 512], replicated, may hold values from -0.25 to 0.25
- w_point: bfloat16 [512, 512], replicated, may hold values from -0.25 to 0.25
- w_depth: float32 [9, 512], replicated, may hold values from -2 to 2
- cotangent: bfloat16 [128, 2048, 512], P('lat', 'lon'), may hold values from -6 to 6
Outputs:
- latent: bfloat16 [128, 2048, 512], P('lat', 'lon')
- grad_in: float32 [616, 512], replicated
- grad_out: float32 [512, 512], replicated
- grad_point: float32 [512, 512], replicated
- grad_depth: float32 [9, 512], replicated
Inputs may be any that keep to these rules, and one draw needn't show every extreme that they name: `owner`: among the 512 rows of one device at most 8 name the same tile, a bound that some block reaches.
All inputs are finite; a program needn't handle non-finite values.
Results may differ from a plain program's by a relative error of at most 0.007.
Values may be sent and summed in bfloat16 or wider, within the bound.
A program may use at most 64 MiB of HBM per device.

v0:
```python
import jax
import jax.numpy as jnp
from jax import lax
from jax.sharding import PartitionSpec as P

offsets = [(a, b) for a in (-1, 0, 1) for b in (-1, 0, 1)]


def extended(block, sides, width, periodic):
    for axis, dim in sides:
        count = lax.axis_size(axis)
        forward = [(i, i + 1) for i in range(count - 1)]
        if periodic:
            forward.append((count - 1, 0))
        backward = [(target, source) for source, target in forward]
        low = lax.ppermute(
            lax.slice_in_dim(block, block.shape[dim] - width, None, axis=dim), axis, forward
        )
        high = lax.ppermute(lax.slice_in_dim(block, 0, width, axis=dim), axis, backward)
        block = jnp.concatenate([low, block, high], axis=dim)
    return block


def send_out(values, places, tiles, cap):
    width = values.shape[1]
    moved, arrived = (
        lax.all_to_all(
            values.reshape(tiles, cap, width),
            ("lat", "lon"),
            split_axis=0,
            concat_axis=0,
            tiled=True,
        ),
        lax.all_to_all(
            places.reshape(tiles, cap), ("lat", "lon"), split_axis=0, concat_axis=0, tiled=True
        ),
    )
    return (moved.reshape(tiles * cap, width), arrived.reshape(tiles * cap))


def send_back(values, tiles, cap):
    width = values.shape[1]
    moved = lax.all_to_all(
        values.reshape(tiles, cap, width), ("lat", "lon"), split_axis=0, concat_axis=0, tiled=True
    )
    return moved.reshape(tiles * cap, width)


def extend(field):
    wide = extended(field, (("lon", 1),), 1, True)
    return extended(wide, (("lat", 0),), 1, False)


def encode(features, w_in, w_out):
    preact = jnp.dot(features, w_in, preferred_element_type=jnp.float32)
    hidden = jax.nn.silu(preact).astype(jnp.bfloat16)
    embedded = jnp.dot(hidden, w_out, preferred_element_type=jnp.float32).astype(jnp.bfloat16)
    return (preact, hidden, embedded)


def on_device(spectra, owner, cell, w_in, w_out, w_point, w_depth, cotangent):
    tiles = lax.axis_size("lat") * lax.axis_size("lon")
    rows_here = spectra.shape[0]
    cap = max(2, 2 * rows_here // tiles)
    clat, clon, width = cotangent.shape
    cells = clat * clon
    target = owner[:, 0]
    hits = (target[:, None] == jnp.arange(tiles, dtype=jnp.int32)[None, :]).astype(jnp.int32)
    position = jnp.sum(jnp.cumsum(hits, axis=0) * hits, axis=1) - 1
    slot_index = target * cap + position
    cells_sent = jnp.full((tiles * cap,), -1, jnp.int32).at[slot_index].set(cell)
    preact, hidden, embedded = encode(spectra, w_in, w_out)
    outgoing = jnp.zeros((tiles * cap, width), jnp.bfloat16).at[slot_index].set(embedded)
    arrived, places = send_out(outgoing, cells_sent, tiles, cap)
    one_hot = (places[None, :] == jnp.arange(cells, dtype=jnp.int32)[:, None]).astype(jnp.bfloat16)
    grid_rows = jnp.dot(one_hot, arrived, preferred_element_type=jnp.float32).astype(jnp.bfloat16)
    grid = grid_rows.reshape(clat, clon, width)
    padded = extend(grid).astype(jnp.float32)
    mixed = jnp.zeros((clat, clon, width), jnp.float32)
    for k, (a, b) in enumerate(offsets):
        mixed = mixed + w_depth[k] * padded[1 + a : 1 + a + clat, 1 + b : 1 + b + clon]
    mixed = mixed.astype(jnp.bfloat16)
    mixed_rows = mixed.reshape(cells, width)
    latent = grid_rows.astype(jnp.float32) + jnp.dot(
        mixed_rows, w_point, preferred_element_type=jnp.float32
    )
    latent = latent.astype(jnp.bfloat16).reshape(clat, clon, width)
    cot_rows = cotangent.reshape(cells, width)
    grad_point = lax.dot_general(
        mixed_rows, cot_rows, (((0,), (0,)), ((), ())), preferred_element_type=jnp.float32
    )
    g_mixed = (
        jnp.dot(cot_rows, w_point.T, preferred_element_type=jnp.float32)
        .astype(jnp.bfloat16)
        .reshape(clat, clon, width)
    )
    g_mixed_f = g_mixed.astype(jnp.float32)
    grad_depth = jnp.stack(
        [
            jnp.sum(g_mixed_f * padded[1 + a : 1 + a + clat, 1 + b : 1 + b + clon], axis=(0, 1))
            for a, b in offsets
        ]
    )
    padded_g = extend(g_mixed).astype(jnp.float32)
    g_grid = cotangent.astype(jnp.float32)
    for k, (a, b) in enumerate(offsets):
        g_grid = g_grid + w_depth[k] * padded_g[1 - a : 1 - a + clat, 1 - b : 1 - b + clon]
    g_grid = g_grid.astype(jnp.bfloat16).reshape(cells, width)
    g_arrived = lax.dot_general(
        one_hot, g_grid, (((0,), (0,)), ((), ())), preferred_element_type=jnp.float32
    ).astype(jnp.bfloat16)
    returned = send_back(g_arrived, tiles, cap)
    g_embedded = returned[slot_index]
    grad_out = lax.dot_general(
        hidden, g_embedded, (((0,), (0,)), ((), ())), preferred_element_type=jnp.float32
    )
    g_hidden = jnp.dot(g_embedded, w_out.T, preferred_element_type=jnp.float32)
    sigmoid_pre = jax.nn.sigmoid(preact)
    g_preact = (g_hidden * sigmoid_pre * (1.0 + preact * (1.0 - sigmoid_pre))).astype(jnp.bfloat16)
    grad_in = lax.dot_general(
        spectra, g_preact, (((0,), (0,)), ((), ())), preferred_element_type=jnp.float32
    )
    grad_in, grad_out, grad_point, grad_depth = lax.psum(
        (grad_in, grad_out, grad_point, grad_depth), ("lat", "lon")
    )
    obs_scale = 1.0 / jnp.sqrt(jnp.float32(rows_here * tiles))
    cell_scale = 1.0 / jnp.sqrt(jnp.float32(cells * tiles))
    return (
        latent,
        grad_in * obs_scale,
        grad_out * obs_scale,
        grad_point * cell_scale,
        grad_depth * cell_scale,
    )


def solution(mesh):
    in_specs = (
        P(("lat", "lon"), None),
        P(("lat", "lon"), None),
        P(("lat", "lon")),
        P(),
        P(),
        P(),
        P(),
        P("lat", "lon", None),
    )
    out_specs = (P("lat", "lon", None), P(), P(), P(), P())
    return jax.shard_map(
        on_device, mesh=mesh, in_specs=in_specs, out_specs=out_specs, check_vma=False
    )
```

profile of v0, /device:TPU:1, one launch (start us, length us, event | category | flops | bytes accessed | tf_op | source)
XLA Modules:
  0.0 320.6 jit_solution(1533166710501741193)
XLA Ops:
  10.0 2.6 scatter_custom_fusion
  13.3 11.5 %all-to-all-start = ((s32[128,1,8]{2,1,0:T(1,128)}), s32[128,1,8]{2,1,0:T(1,128)S(1)}, u32[]{:S(2)}, u32[]{:S(2)}) async-start(s32[128,1,8]{2,1,0:T(1,128)} %bitcast.7), calls=%async_computation | async-start | bytes 131072 | tf_op jit(solution)/shard_map/all_to_all | solution.py:34
  24.8 2.7 fusion.46
  27.5 1.7 convolution_convert_fusion.1
  29.2 3.5 %scatter_custom_fusion.1 = bf16[1024,512]{1,0:T(8,128)(2,1)} fusion(s32[512]{0:T(512)S(1)} %bitcast.109, bf16[512,512]{1,0:T(8,128)(2,1)S(1)} %convolution_convert_fusion.1, bf16[]{:T(256)} %constant.13.clone.1), kind=kCustom, calls=%fused_computation.69 | custom fusion | bytes 1048578 | tf_op jit(solution)/shard_map/scatter | solution.py:73
  32.6 1.9 all-to-all-done
  34.5 7.9 %all-to-all-start.1 = ((bf16[128,8,512]{2,1,0:T(8,128)(2,1)}), bf16[128,8,512]{2,1,0:T(8,128)(2,1)S(1)}, u32[]{:S(2)}, u32[]{:S(2)}) async-start(bf16[128,8,512]{2,1,0:T(8,128)(2,1)} %bitcast.8), calls=%async_computation.1 | async-start | bytes 2097152 | tf_op jit(solution)/shard_map/all_to_all | solution.py:27
  43.8 17.4 %all-to-all-done.1 = bf16[128,8,512]{2,1,0:T(8,128)(2,1)S(1)} async-done(((bf16[128,8,512]{2,1,0:T(8,128)(2,1)}), bf16[128,8,512]{2,1,0:T(8,128)(2,1)S(1)}, u32[]{:S(2)}, u32[]{:S(2)}) %all-to-all-start.1) | async-done | bytes 1048608 | tf_op jit(solution)/shard_map/all_to_all | solution.py:27
  61.2 2.3 fusion.23
  64.4 4.2 %collective-permute-start.1 = (bf16[16,1,512]{2,1,0:T(2,128)(2,1)S(1)}, bf16[16,1,512]{2,1,0:T(2,128)(2,1)S(1)}, u32[]{:S(2)}, u32[]{:S(2)}) collective-permute-start(bf16[16,1,512]{2,1,0:T(2,128)(2,1)S(1)} %get-tuple-element.24), channel_id=1, source_target_pairs={{1,0},{2,1},{3,2},{4,3},{5,4},{6,5},{7,6},{8,7},{9,8},{10,9},{11,1... | collective-permute-start | bytes 49160 | tf_op jit(solution)/shard_map/ppermute | solution.py:19
  68.5 1.3 collective-permute-done
  69.9 4.6 %collective-permute-start.2 = (bf16[1,130,512]{2,1,0:T(8,128)(2,1)S(1)}, bf16[1,130,512]{2,1,0:T(8,128)(2,1)S(1)}, u32[]{:S(2)}, u32[]{:S(2)}) collective-permute-start(bf16[1,130,512]{2,1,0:T(8,128)(2,1)S(1)} %get-tuple-element.19), channel_id=1, source_target_pairs={{0,16},{16,32},{32,48},{48,64},{64,80},{80,96},{96,112},{1,17},{17... | collective-permute-start | bytes 399368 | tf_op jit(solution)/shard_map/ppermute | solution.py:16
  74.5 2.1 collective-permute-start.3
  76.7 4.3 %collective-permute-done.3 = bf16[1,130,512]{2,1,0:T(8,128)(2,1)S(1)} collective-permute-done((bf16[1,130,512]{2,1,0:T(8,128)(2,1)S(1)}, bf16[1,130,512]{2,1,0:T(8,128)(2,1)S(1)}, u32[]{:S(2)}, u32[]{:S(2)}) %collective-permute-start.3) | collective-permute-done | bytes 133152 | tf_op jit(solution)/shard_map/ppermute | solution.py:19
  81.8 8.6 %fusion.10 = (f32[512]{0:T(512)S(1)}, f32[512]{0:T(512)S(1)}, f32[512]{0:T(512)S(1)}, f32[512]{0:T(512)S(1)}, f32[512]{0:T(512)S(1)}, /*index=5*/f32[512]{0:T(51...) fusion(f32[18,130,512]{2,1,0:T(8,128)S(1)} %maximum_convert_fusion, ...), kind=kOutput, calls=%fused_computation.23 | convolution fusion | flops 1094708736 | bytes 42485760 | tf_op jit(solution)/shard_map/dot_general | solution.py:93
  90.6 5.1 %collective-permute-start.5 = (bf16[16,1,512]{2,1,0:T(2,128)(2,1)S(1)}, bf16[16,1,512]{2,1,0:T(2,128)(2,1)S(1)}, u32[]{:S(2)}, u32[]{:S(2)}) collective-permute-start(bf16[16,1,512]{2,1,0:T(2,128)(2,1)S(1)} %get-tuple-element.22), channel_id=1, source_target_pairs={{1,0},{2,1},{3,2},{4,3},{5,4},{6,5},{7,6},{8,7},{9,8},{10,9},{11,1... | collective-permute-start | bytes 49160 | tf_op jit(solution)/shard_map/ppermute | solution.py:19
  97.0 2.8 collective-permute-start.6
  99.8 1.9 collective-permute-start.7
  101.8 4.4 %collective-permute-done.7 = bf16[1,130,512]{2,1,0:T(8,128)(2,1)S(1)} collective-permute-done((bf16[1,130,512]{2,1,0:T(8,128)(2,1)S(1)}, bf16[1,130,512]{2,1,0:T(8,128)(2,1)S(1)}, u32[]{:S(2)}, u32[]{:S(2)}) %collective-permute-start.7) | collective-permute-done | bytes 133152 | tf_op jit(solution)/shard_map/ppermute | solution.py:19
  107.1 5.4 %fusion.12 = bf16[16,128,512]{2,1,0:T(8,128)(2,1)S(1)} fusion(f32[18,130,512]{2,1,0:T(8,128)S(1)} %maximum_convert_fusion.1, bf16[16,128,512]{2,1,0:T(8,128)(2,1)S(1)} %copy-done.4, f32[512]{0:T(512)S(1)} %bitcast.101, f32[512]{0:T(512)S(1)} %bitcast.103, f32[512]{0:T(512)S(1)} %bitcast.89, f32[512]{0:T(512)S(1)} %bitcast.91, f32[512]{0:T(512)S(1)} %bitcast.93, ...), kind=kLoop, calls=%fused_computation.26 | loop fusion | flops 20971520 | bytes 41961472 | tf_op jit(solution)/shard_map/convert_element_type | solution.py:108
  112.5 3.3 %fusion.25 = bf16[128,8,512]{2,1,0:T(8,128)(2,1)} fusion(bf16[2048,512]{1,0:T(8,128)(2,1)S(1)} %bitcast.84, s32[1024]{0:T(1024)S(1)} %eq.48), kind=kOutput, calls=%fused_computation.53 | convolution fusion | flops 2150105088 | bytes 3149824 | tf_op jit(solution)/shard_map/dot_general | solution.py:109
  115.8 7.9 %all-to-all-start.2 = ((bf16[128,8,512]{2,1,0:T(8,128)(2,1)}), bf16[128,8,512]{2,1,0:T(8,128)(2,1)S(1)}, u32[]{:S(2)}, u32[]{:S(2)}) async-start(bf16[128,8,512]{2,1,0:T(8,128)(2,1)} %fusion.25), calls=%async_computation.2 | async-start | bytes 2097152 | tf_op jit(solution)/shard_map/all_to_all | solution.py:43
  124.0 17.2 %add_convert_fusion.1 = bf16[16,128,512]{2,1,0:T(8,128)(2,1)} fusion(f32[18,130,512]{2,1,0:T(8,128)} %copy-done.1, f32[512]{0:T(512)S(1)} %bitcast.102, f32[512]{0:T(512)S(1)} %bitcast.104, f32[512]{0:T(512)S(1)} %bitcast.90, f32[512]{0:T(512)S(1)} %bitcast.92, f32[512]{0:T(512)S(1)} %bitcast.94, f32[512]{0:T(512)S(1)} %bitcast.96, f32[512]{0:T(512)S(1)} %bitcast.98, ...), kind=kLoop, calls=%fused_computation.44 | loop fusion | flops 18874368 | bytes 39864320 | tf_op jit(solution)/shard_map/convert_element_type | solution.py:82
  141.2 3.9 %convolution_bitcast_fusion.1 = f32[512,512]{1,0:T(8,128)} fusion(bf16[16,128,512]{2,1,0:T(8,128)(2,1)} %add_convert_fusion.1, bf16[16,128,512]{2,1,0:T(8,128)(2,1)S(1)} %copy-done.5), kind=kOutput, calls=%fused_computation.54 | convolution fusion | flops 1073741824 | bytes 5242880 | tf_op jit(solution)/shard_map/dot_general | solution.py:89
  145.0 2.0 gather_fusion
  147.0 2.7 fusion.42
  149.7 3.6 %convolution_bitcast_fusion = f32[616,512]{1,0:T(8,128)} fusion(bf16[512,616]{0,1:T(8,128)(2,1)S(1)} %copy-done, bf16[512,512]{1,0:T(8,128)(2,1)S(1)} %gather_fusion, bf16[512,512]{1,0:T(8,128)(2,1)} %param.12, f32[512,512]{1,0:T(8,128)} %fusion.46), kind=kOutput, calls=%fused_computation.52 | convolution fusion | flops 593756160 | bytes 3989504 | tf_op jit(solution)/shard_map/dot_general | solution.py:120
  153.4 67.8 %psum.31 = f32[9,512]{1,0:T(8,128)S(1)} all-reduce(f32[9,512]{1,0:T(8,128)S(1)} %stack.39), channel_id=1, replica_groups=mesh['lat'=8,'lon'=16] {'lat','lon'}, use_global_device_ids=true, to_apply=%region_17.18 | all-reduce | flops 4608 | bytes 36864 | tf_op jit(solution)/shard_map/psum | solution.py:123
  221.8 4.3 %add_convert_fusion = bf16[2048,512]{1,0:T(8,128)(2,1)} fusion(bf16[2048,512]{1,0:T(8,128)(2,1)S(1)} %copy-done.3, bf16[2048,512]{1,0:T(8,128)(2,1)} %bitcast.20, bf16[512,512]{1,0:T(8,128)(2,1)} %param.13), kind=kOutput, calls=%fused_computation.43 | convolution fusion | flops 1076887552 | bytes 6815744 | tf_op jit(solution)/shard_map/dot_general | solution.py:84
  226.1 82.1 %all-reduce.3.cloned.1.call-done = (f32[616,512]{1,0:T(8,128)}, f32[512,512]{1,0:T(8,128)}, f32[512,512]{1,0:T(8,128)}) async-done(((f32[616,512]{1,0:T(8,128)}, f32[512,512]{1,0:T(8,128)}, f32[512,512]{1,0:T(8,128)}), (f32[616,512]{1,0:T(8,128)}, f32[512,512]{1,0:T(8,128)}, f32[512,512]{1,0:T(8,128)})) %all-reduce.3.cloned.1.call-update) | async-done | bytes 3358736 | tf_op jit(solution)/shard_map/psum | solution.py:123
  308.2 2.5 broadcast_multiply_fusion
  310.7 3.1 broadcast_multiply_fusion.1
  (51 shorter events, 9.9 us)
Async XLA Ops:
  7.2 17.7 %copy-start = (bf16[512,616]{0,1:T(8,128)(2,1)S(1)}, bf16[512,616]{0,1:T(8,128)(2,1)}, u32[]{:S(2)}) copy-start(bf16[512,616]{0,1:T(8,128)(2,1)} %param.8) | copy-start | bytes 1892356
  7.2 20.3 %copy-start.7 = (bf16[512,512]{1,0:T(8,128)(2,1)S(1)}, bf16[512,512]{1,0:T(8,128)(2,1)}, u32[]{:S(2)}) copy-start(bf16[512,512]{1,0:T(8,128)(2,1)} %param.12) | copy-start | bytes 1572868
  13.3 21.2 %all-to-all-start = ((s32[128,1,8]{2,1,0:T(1,128)}), s32[128,1,8]{2,1,0:T(1,128)S(1)}, u32[]{:S(2)}, u32[]{:S(2)}) async-start(s32[128,1,8]{2,1,0:T(1,128)} %bitcast.7), calls=%async_computation | async-start | bytes 131072 | tf_op jit(solution)/shard_map/all_to_all | solution.py:34
  34.5 26.7 %all-to-all-start.1 = ((bf16[128,8,512]{2,1,0:T(8,128)(2,1)}), bf16[128,8,512]{2,1,0:T(8,128)(2,1)S(1)}, u32[]{:S(2)}, u32[]{:S(2)}) async-start(bf16[128,8,512]{2,1,0:T(8,128)(2,1)} %bitcast.8), calls=%async_computation.1 | async-start | bytes 2097152 | tf_op jit(solution)/shard_map/all_to_all | solution.py:27
  63.6 18.2 %copy-start.2 = (bf16[2048,512]{1,0:T(8,128)(2,1)}, bf16[2048,512]{1,0:T(8,128)(2,1)S(1)}, u32[]{:S(2)}) copy-start(bf16[2048,512]{1,0:T(8,128)(2,1)S(1)} %fusion.23) | copy-start | bytes 6291460
  63.7 6.2 %collective-permute-start = (bf16[16,1,512]{2,1,0:T(2,128)(2,1)S(1)}, bf16[16,1,512]{2,1,0:T(2,128)(2,1)S(1)}, u32[]{:S(2)}, u32[]{:S(2)}) collective-permute-start(bf16[16,1,512]{2,1,0:T(2,128)(2,1)S(1)} %get-tuple-element.23), channel_id=1, source_target_pairs={{0,1},{1,2},{2,3},{3,4},{4,5},{5,6},{6,7},{7,8},{8,9},{9,10},{10,1... | collective-permute-start | bytes 49160 | tf_op jit(solution)/shard_map/ppermute | solution.py:16
  64.4 5.5 %collective-permute-start.1 = (bf16[16,1,512]{2,1,0:T(2,128)(2,1)S(1)}, bf16[16,1,512]{2,1,0:T(2,128)(2,1)S(1)}, u32[]{:S(2)}, u32[]{:S(2)}) collective-permute-start(bf16[16,1,512]{2,1,0:T(2,128)(2,1)S(1)} %get-tuple-element.24), channel_id=1, source_target_pairs={{1,0},{2,1},{3,2},{4,3},{5,4},{6,5},{7,6},{8,7},{9,8},{10,9},{11,1... | collective-permute-start | bytes 49160 | tf_op jit(solution)/shard_map/ppermute | solution.py:19
  69.9 6.7 %collective-permute-start.2 = (bf16[1,130,512]{2,1,0:T(8,128)(2,1)S(1)}, bf16[1,130,512]{2,1,0:T(8,128)(2,1)S(1)}, u32[]{:S(2)}, u32[]{:S(2)}) collective-permute-start(bf16[1,130,512]{2,1,0:T(8,128)(2,1)S(1)} %get-tuple-element.19), channel_id=1, source_target_pairs={{0,16},{16,32},{32,48},{48,64},{64,80},{80,96},{96,112},{1,17},{17... | collective-permute-start | bytes 399368 | tf_op jit(solution)/shard_map/ppermute | solution.py:16
  74.5 6.4 %collective-permute-start.3 = (bf16[1,130,512]{2,1,0:T(8,128)(2,1)S(1)}, bf16[1,130,512]{2,1,0:T(8,128)(2,1)S(1)}, u32[]{:S(2)}, u32[]{:S(2)}) collective-permute-start(bf16[1,130,512]{2,1,0:T(8,128)(2,1)S(1)} %get-tuple-element.20), channel_id=1, source_target_pairs={{16,0},{32,16},{48,32},{64,48},{80,64},{96,80},{112,96},{17,1},{33... | collective-permute-start | bytes 399368 | tf_op jit(solution)/shard_map/ppermute | solution.py:19
  81.8 8.6 %copy-start.1 = (f32[18,130,512]{2,1,0:T(8,128)}, f32[18,130,512]{2,1,0:T(8,128)S(1)}, u32[]{:S(2)}) copy-start(f32[18,130,512]{2,1,0:T(8,128)S(1)} %maximum_convert_fusion) | copy-start | bytes 14376964
  81.8 19.9 %copy-start.6 = (f32[9,512]{1,0:T(8,128)S(1)}, f32[9,512]{1,0:T(8,128)}, u32[]{:S(2)}) copy-start(f32[9,512]{1,0:T(8,128)} %param.14) | copy-start | bytes 55300
  90.5 6.4 %collective-permute-start.4 = (bf16[16,1,512]{2,1,0:T(2,128)(2,1)S(1)}, bf16[16,1,512]{2,1,0:T(2,128)(2,1)S(1)}, u32[]{:S(2)}, u32[]{:S(2)}) collective-permute-start(bf16[16,1,512]{2,1,0:T(2,128)(2,1)S(1)} %get-tuple-element.21), channel_id=1, source_target_pairs={{0,1},{1,2},{2,3},{3,4},{4,5},{5,6},{6,7},{7,8},{8,9},{9,10},{10,1... | collective-permute-start | bytes 49160 | tf_op jit(solution)/shard_map/ppermute | solution.py:16
  90.6 6.4 %collective-permute-start.5 = (bf16[16,1,512]{2,1,0:T(2,128)(2,1)S(1)}, bf16[16,1,512]{2,1,0:T(2,128)(2,1)S(1)}, u32[]{:S(2)}, u32[]{:S(2)}) collective-permute-start(bf16[16,1,512]{2,1,0:T(2,128)(2,1)S(1)} %get-tuple-element.22), channel_id=1, source_target_pairs={{1,0},{2,1},{3,2},{4,3},{5,4},{6,5},{7,6},{8,7},{9,8},{10,9},{11,1... | collective-permute-start | bytes 49160 | tf_op jit(solution)/shard_map/ppermute | solution.py:19
  97.0 10.0 %copy-start.4 = (bf16[16,128,512]{2,1,0:T(8,128)(2,1)S(1)}, bf16[16,128,512]{2,1,0:T(8,128)(2,1)}, u32[]{:S(2)}) copy-start(bf16[16,128,512]{2,1,0:T(8,128)(2,1)} %param.15) | copy-start | bytes 6291460
  97.0 4.8 %collective-permute-start.6 = (bf16[1,130,512]{2,1,0:T(8,128)(2,1)S(1)}, bf16[1,130,512]{2,1,0:T(8,128)(2,1)S(1)}, u32[]{:S(2)}, u32[]{:S(2)}) collective-permute-start(bf16[1,130,512]{2,1,0:T(8,128)(2,1)S(1)} %get-tuple-element.17), channel_id=1, source_target_pairs={{0,16},{16,32},{32,48},{48,64},{64,80},{80,96},{96,112},{1,17},{17... | collective-permute-start | bytes 399368 | tf_op jit(solution)/shard_map/ppermute | solution.py:16
  99.8 6.4 %collective-permute-start.7 = (bf16[1,130,512]{2,1,0:T(8,128)(2,1)S(1)}, bf16[1,130,512]{2,1,0:T(8,128)(2,1)S(1)}, u32[]{:S(2)}, u32[]{:S(2)}) collective-permute-start(bf16[1,130,512]{2,1,0:T(8,128)(2,1)S(1)} %get-tuple-element.18), channel_id=1, source_target_pairs={{16,0},{32,16},{48,32},{64,48},{80,64},{96,80},{112,96},{17,1},{33... | collective-permute-start | bytes 399368 | tf_op jit(solution)/shard_map/ppermute | solution.py:19
  115.8 29.2 %all-to-all-start.2 = ((bf16[128,8,512]{2,1,0:T(8,128)(2,1)}), bf16[128,8,512]{2,1,0:T(8,128)(2,1)S(1)}, u32[]{:S(2)}, u32[]{:S(2)}) async-start(bf16[128,8,512]{2,1,0:T(8,128)(2,1)} %fusion.25), calls=%async_computation.2 | async-start | bytes 2097152 | tf_op jit(solution)/shard_map/all_to_all | solution.py:43
  123.7 184.5 %all-reduce.3.cloned.1.call-start = ((), (), s32[]{:S(2)}) async-start(), calls=%async_computation.3 | async-start | bytes 6717440 | tf_op jit(solution)/shard_map/psum | solution.py:123
  124.0 17.2 %copy-start.5 = (bf16[16,128,512]{2,1,0:T(8,128)(2,1)S(1)}, bf16[16,128,512]{2,1,0:T(8,128)(2,1)}, u32[]{:S(2)}) copy-start(bf16[16,128,512]{2,1,0:T(8,128)(2,1)} %param.15) | copy-start | bytes 6291460
  149.7 72.1 %copy-start.3 = (bf16[2048,512]{1,0:T(8,128)(2,1)S(1)}, bf16[2048,512]{1,0:T(8,128)(2,1)}, u32[]{:S(2)}) copy-start(bf16[2048,512]{1,0:T(8,128)(2,1)} %copy-done.2) | copy-start | bytes 6291460
Sparse Core Ops, SparseCore 0:
  153.4 154.7 all-reduce.2
where the time goes:
time: 321 us
  waiting for transfers between devices  113 us (35%)
  blocking collectives  67.8 us (21%)
  starting transfers between devices  49 us (15%)
  other arithmetic  33.3 us (10%)
  matrix products  33 us (10%)
  between operations  14.4 us (4%)
  local copies, waits for them, and re-layouts  10.5 us (3%)
    psum x1, waiting for transfers between devices, on_device(): lax.psum((grad_in, grad_out, grad_point, grad_depth), ('lat', 'lon'))  82.1 us
    psum x1, blocking collectives, on_device(): lax.psum((grad_in, grad_out, grad_point, grad_depth), ('lat', 'lon'))  67.8 us
    all_to_all x1, waiting for transfers between devices, send_out(): lax.all_to_all(values.reshape(tiles, cap, width), ('lat', 'lon'), split_a...  17.4 us
    convert_element_type x1, other arithmetic, on_device(): mixed = mixed.astype(jnp.bfloat16)  17.2 us
    ppermute x4, starting transfers between devices, extended(): lax.ppermute(lax.slice_in_dim(block, 0, width, axis=dim), axis, backward)  13.3 us
    all_to_all x1, starting transfers between devices, send_out(): lax.all_to_all(places.reshape(tiles, cap), ('lat', 'lon'), split_axis=0,...  11.5 us
    ppermute x4, waiting for transfers between devices, extended(): lax.ppermute(lax.slice_in_dim(block, 0, width, axis=dim), axis, backward)  8.63 us
    dot_general x1, matrix products, on_device(): jnp.dot(cot_rows, w_point.T, preferred_element_type=jnp.float32)  8.6 us
  transfers between devices with their start and end apart: 12, of which 7 were waited for; matrix products, arithmetic and copies ran while one was open for 11% of the time, Pallas kernels for 0%

commit v1 on v0

v1 whole, which is shorter than its diff:
```python
import functools

import jax
import jax.numpy as jnp
from jax import lax
from jax.experimental import pallas as pl
from jax.experimental.pallas import tpu as pltpu
from jax.sharding import PartitionSpec as P

offsets = [(a, b) for a in (-1, 0, 1) for b in (-1, 0, 1)]
f32, bf16, i32 = jnp.float32, jnp.bfloat16, jnp.int32

N_LAT, N_LON, SIDE = 8, 16, 4
CHIPS = N_LAT // 2 * N_LON
CAP = 8
SLOT = 2 * CAP
SLOTS = CHIPS * SLOT
OBS = 512
C = 512
CLAT, CLON = 16, 128
CELLS = CLAT * CLON
SPEC = 616
META = 128
ROWS_IN = 624
ROWS = ROWS_IN + C + C + 16
BLOCKS = ROWS // 16
HALF = BLOCKS // 2
HALF_ROWS = HALF * 16

VMEM = pltpu.VMEM


def vmem():
    return pl.BlockSpec(memory_space=pltpu.VMEM)


def dot(a, b, dims):
    return lax.dot_general(a, b, (dims, ((), ())), preferred_element_type=f32)


class Place:
    def __init__(self):
        self.lat = lax.axis_index("lat")
        self.lon = lax.axis_index("lon")
        self.core = self.lat % 2
        self.x = self.lat // 2
        self.chip = self.x * N_LON + self.lon
        self.sibling = (self.x * 2 + 1 - self.core, self.lon)

    def peer(self, step):
        step = (step * 37) % CHIPS
        x = (self.x + step // N_LON) % (N_LAT // 2)
        z = (self.lon // SIDE + step // SIDE) % SIDE
        y = (self.lon + step) % SIDE
        lon = z * SIDE + y
        return x * N_LON + lon, (x * 2 + self.core, lon)

    def of_chip(self, chip):
        return (chip // N_LON * 2 + self.core, chip % N_LON)


def remote(src, dst, send, recv, device):
    return pltpu.make_async_remote_copy(
        src_ref=src,
        dst_ref=dst,
        send_sem=send,
        recv_sem=recv,
        device_id=device,
        device_id_type=pl.DeviceIdType.MESH,
    )


def greet(place, halo):
    barrier = pltpu.get_barrier_semaphore()

    def hello(device):
        pl.semaphore_signal(
            barrier, inc=1, device_id=device, device_id_type=pl.DeviceIdType.MESH
        )

    def one(step, carry):
        hello(place.peer(step)[1])
        return carry

    lax.fori_loop(1, CHIPS, one, 0)
    if not halo:
        hello(place.sibling)
        return barrier, CHIPS
    for side in (-1, 1):
        inside = (place.lat + side >= 0) & (place.lat + side < N_LAT)

        @pl.when(inside)
        def _(side=side):
            for turn in (-1, 0, 1):
                hello((place.lat + side, (place.lon + turn + N_LON) % N_LON))

    edges = (place.lat > 0).astype(i32) + (place.lat < N_LAT - 1).astype(i32)
    return barrier, CHIPS - 1 + 3 * edges


class Halo:
    def __init__(self, place, rows, cols, to_rows, to_cols, to_diag, send, recv):
        self.place = place
        self.outs = (to_rows, to_diag)
        lat, lon = place.lat, place.lon
        east, west = (lon + 1) % N_LON, (lon + N_LON - 1) % N_LON
        has_north, has_south = lat > 0, lat < N_LAT - 1
        south, north = jnp.minimum(lat + 1, N_LAT - 1), jnp.maximum(lat - 1, 0)
        plan = [
            (rows.at[1], to_rows.at[0], (south, lon), has_south, has_north),
            (rows.at[0], to_rows.at[1], (north, lon), has_north, has_south),
            (cols.at[1], to_cols.at[0], (lat, east), None, None),
            (cols.at[0], to_cols.at[1], (lat, west), None, None),
            (cols.at[1], to_diag.at[0], (south, east), has_south, has_north),
            (cols.at[0], to_diag.at[1], (south, west), has_south, has_north),
            (cols.at[1], to_diag.at[2], (north, east), has_north, has_south),
            (cols.at[0], to_diag.at[3], (north, west), has_north, has_south),
        ]
        self.plan = [
            (remote(src, dst, send.at[i], recv.at[i], device), sends, receives)
            for i, (src, dst, device, sends, receives) in enumerate(plan)
        ]

    def start(self):
        for copy, sends, _ in self.plan:
            if sends is None:
                copy.start()
            else:
                pl.when(sends)(copy.start)

    def wait(self):
        for copy, sends, receives in self.plan:
            if sends is None:
                copy.wait_send()
                copy.wait_recv()
            else:
                pl.when(sends)(copy.wait_send)
                pl.when(receives)(copy.wait_recv)

    def clear_outside(self):
        rows, diag = self.outs

        @pl.when(self.place.lat == 0)
        def _():
            rows[0] = jnp.zeros_like(rows[0])
            diag[0] = jnp.zeros_like(diag[0])
            diag[1] = jnp.zeros_like(diag[1])

        @pl.when(self.place.lat == N_LAT - 1)
        def _():
            rows[1] = jnp.zeros_like(rows[1])
            diag[2] = jnp.zeros_like(diag[2])
            diag[3] = jnp.zeros_like(diag[3])


HALO_OUT = [
    jax.ShapeDtypeStruct((2, CLON, C), bf16),
    jax.ShapeDtypeStruct((2, CLAT, C), bf16),
    jax.ShapeDtypeStruct((4, CLAT, C), bf16),
]


def encode_kernel(spec_t, rows, w_in, w_out, preact, hidden, emb, route):
    pre = dot(spec_t[...], w_in[...], ((0,), (0,)))
    preact[...] = pre
    hid = (pre * (1.0 / (1.0 + jnp.exp(-pre)))).astype(bf16)
    hidden[...] = hid
    emb[:, :C] = dot(hid, w_out[...], ((1,), (0,))).astype(bf16)
    values = rows[...]
    down = lax.broadcasted_iota(i32, (OBS, OBS), 0)
    across = lax.broadcasted_iota(i32, (OBS, OBS), 1)
    eye = (down == across).astype(f32).astype(bf16)
    columns = dot(eye, values, ((1,), (1,)))
    tile_col, high_col, low_col = columns[:, 0:1], columns[:, 1:2], columns[:, 2:3]
    tile_row = values[0:1, :].astype(f32)
    tiles = N_LAT * N_LON
    hits = (tile_col == lax.broadcasted_iota(i32, (OBS, tiles), 1).astype(f32)).astype(f32)
    lower = (across <= down).astype(f32).astype(bf16)
    count = dot(lower, hits.astype(bf16), ((1,), (0,)))
    pos_col = (jnp.sum(count * hits, axis=1, keepdims=True) - 1.0).astype(i32)
    hits_t = (tile_row == lax.broadcasted_iota(i32, (tiles, OBS), 0).astype(f32)).astype(f32)
    upper = (down <= across).astype(f32).astype(bf16)
    count_t = dot(hits_t.astype(bf16), upper, ((1,), (0,)))
    pos_row = (jnp.sum(count_t * hits_t, axis=0, keepdims=True) - 1.0).astype(i32)
    lane = lax.broadcasted_iota(i32, (OBS, META), 1)
    kind = lane // CAP
    value = jnp.where(kind == 0, high_col, jnp.where(kind == 1, low_col, 1.0))
    keep = (lane % CAP == pos_col) & (kind < 3)
    emb[:, C:] = jnp.where(keep, value, 0.0).astype(bf16)
    tile = tile_row.astype(i32)
    lat, lon = tile // N_LON, tile % N_LON
    chip = lat // 2 * N_LON + lon
    route[...] = jnp.concatenate(
        [chip * SLOT + pos_row, lat % 2, chip, jnp.zeros((5, OBS), i32)], axis=0
    )


def encode(spec_t, rows, w_in, w_out):
    return pl.pallas_call(
        encode_kernel,
        out_shape=[
            jax.ShapeDtypeStruct((OBS, C), f32),
            jax.ShapeDtypeStruct((OBS, C), bf16),
            jax.ShapeDtypeStruct((OBS, C + META), bf16),
            jax.ShapeDtypeStruct((8, OBS), i32),
        ],
        in_specs=[vmem()] * 4,
        out_specs=[vmem()] * 4,
        compiler_params=pltpu.CompilerParams(vmem_limit_bytes=40 << 20),
    )(spec_t, rows, w_in, w_out)


def slot_keys(route, mine, core):
    return jnp.where(route[1:2, :] == mine, route[0:1, :] + CAP * core, -1)


PART = 256


def forward_kernel(
    emb,
    route,
    rows,
    cols,
    arrived,
    places,
    route_sib,
    to_rows,
    to_cols,
    to_diag,
    emb_sib,
    outgoing,
    marks,
    local_sem,
    sib_send,
    sib_recv,
    data_send,
    data_recv,
    halo_send,
    halo_recv,
):
    place = Place()
    core = place.core
    barrier, count = greet(place, True)
    halo = Halo(place, rows, cols, to_rows, to_cols, to_diag, halo_send, halo_recv)
    halo.clear_outside()
    pl.semaphore_wait(barrier, count)
    swaps = [
        remote(emb, emb_sib, sib_send.at[0], sib_recv.at[0], place.sibling),
        remote(route, route_sib, sib_send.at[1], sib_recv.at[1], place.sibling),
    ]
    for copy in swaps:
        copy.start()
    halo.start()
    key = slot_keys(route[...], core, core)

    def own_part(i, carry):
        at = pl.multiple_of(i * PART, PART)
        index = lax.broadcasted_iota(i32, (PART, OBS), 0) + at
        pick = (index == key).astype(f32).astype(bf16)
        outgoing[pl.ds(at, PART), :] = dot(pick, emb[:, :C], ((1,), (0,))).astype(bf16)
        return carry

    lax.fori_loop(0, SLOTS // PART, own_part, 0)
    for copy in swaps:
        copy.wait()
    key_sib = slot_keys(route_sib[...], core, 1 - core)

    def sib_part(i, carry):
        at = pl.multiple_of(i * PART, PART)
        index = lax.broadcasted_iota(i32, (PART, OBS), 0) + at
        pick = (index == key_sib).astype(f32).astype(bf16)
        more = dot(pick, emb_sib[:, :C], ((1,), (0,)))
        outgoing[pl.ds(at, PART), :] = (
            outgoing[pl.ds(at, PART), :].astype(f32) + more
        ).astype(bf16)
        return carry

    lax.fori_loop(0, SLOTS // PART, sib_part, 0)
    chips = lax.broadcasted_iota(i32, (CHIPS, OBS), 0)

    def marked(info, values):
        wanted = (info[2:3, :] == chips) & (info[1:2, :] == core)
        return dot(wanted.astype(f32).astype(bf16), values[:, C:], ((1,), (0,)))

    own, other = marked(route, emb), marked(route_sib, emb_sib)
    marks[:, 0, :] = jnp.where(core == 0, own, other)
    marks[:, 1, :] = jnp.where(core == 0, other, own)

    def block(ref, chip):
        return ref.at[pl.ds(pl.multiple_of(chip * SLOT, SLOT), SLOT)]

    keep = [
        pltpu.make_async_copy(block(outgoing, place.chip), block(arrived, place.chip), local_sem.at[0]),
        pltpu.make_async_copy(marks.at[place.chip], places.at[place.chip], local_sem.at[1]),
    ]
    for copy in keep:
        copy.start()

    def send(step, carry):
        chip, device = place.peer(step)
        remote(
            marks.at[chip], places.at[place.chip], data_send.at[1], data_recv.at[1], device
        ).start()
        remote(
            block(outgoing, chip),
            block(arrived, place.chip),
            data_send.at[0],
            data_recv.at[0],
            device,
        ).start()
        return carry

    lax.fori_loop(1, CHIPS, send, 0)
    for copy in keep:
        copy.wait()
    halo.wait()
    some = pl.ds(0, (CHIPS - 1) * SLOT)
    whole = [
        remote(
            outgoing.at[some], arrived.at[some], data_send.at[0], data_recv.at[0], place.sibling
        ),
        remote(
            marks.at[pl.ds(0, CHIPS - 1)],
            places.at[pl.ds(0, CHIPS - 1)],
            data_send.at[1],
            data_recv.at[1],
            place.sibling,
        ),
    ]
    for copy in whole:
        copy.wait_recv()
        copy.wait_send()


def forward_exchange(emb, route, rows, cols):
    dma = pltpu.SemaphoreType.DMA
    return pl.pallas_call(
        forward_kernel,
        out_shape=[
            jax.ShapeDtypeStruct((SLOTS, C), bf16),
            jax.ShapeDtypeStruct((CHIPS, 2, META), f32),
            jax.ShapeDtypeStruct((8, OBS), i32),
        ]
        + HALO_OUT,
        in_specs=[vmem()] * 4,
        out_specs=[vmem()] * 6,
        scratch_shapes=[
            VMEM((OBS, C + META), bf16),
            VMEM((SLOTS, C), bf16),
            VMEM((CHIPS, 2, META), f32),
            dma((2,)),
            dma((2,)),
            dma((2,)),
            dma((2,)),
            dma((2,)),
            dma((8,)),
            dma((8,)),
        ],
        compiler_params=pltpu.CompilerParams(
            collective_id=0, has_side_effects=True, vmem_limit_bytes=40 << 20
        ),
    )(emb, route, rows, cols)


def backward_kernel(
    grads,
    route,
    route_sib,
    rows,
    cols,
    result,
    to_rows,
    to_cols,
    to_diag,
    returned,
    part,
    part_sib,
    local_sem,
    sib_send,
    sib_recv,
    data_send,
    data_recv,
    halo_send,
    halo_recv,
):
    place = Place()
    core = place.core
    barrier, count = greet(place, True)
    halo = Halo(place, rows, cols, to_rows, to_cols, to_diag, halo_send, halo_recv)
    halo.clear_outside()
    pl.semaphore_wait(barrier, count)
    halo.start()

    def block(ref, chip):
        return ref.at[pl.ds(pl.multiple_of(chip * SLOT, SLOT), SLOT)]

    keep = pltpu.make_async_copy(
        block(grads, place.chip), block(returned, place.chip), local_sem.at[0]
    )
    keep.start()

    def send(step, carry):
        chip, device = place.peer(step)
        remote(
            block(grads, chip),
            block(returned, place.chip),
            data_send.at[0],
            data_recv.at[0],
            device,
        ).start()
        return carry

    lax.fori_loop(1, CHIPS, send, 0)
    keep.wait()
    halo.wait()
    some = pl.ds(0, (CHIPS - 1) * SLOT)
    whole = remote(
        grads.at[some], returned.at[some], data_send.at[0], data_recv.at[0], place.sibling
    )
    whole.wait_recv()
    whole.wait_send()

    def gathered(key):
        total = jnp.zeros((OBS, C), f32)
        for at in range(0, SLOTS, PART):
            index = lax.broadcasted_iota(i32, (PART, OBS), 0) + at
            pick = (index == key).astype(f32).astype(bf16)
            total = total + dot(pick, returned[at : at + PART, :], ((0,), (0,)))
        return total

    part[...] = gathered(slot_keys(route_sib[...], core, 1 - core)).astype(bf16)
    swap = remote(part, part_sib, sib_send.at[0], sib_recv.at[0], place.sibling)
    swap.start()
    own = gathered(slot_keys(route[...], core, core))
    swap.wait()
    result[...] = (own + part_sib[...].astype(f32)).astype(bf16)


def backward_exchange(grads, route, route_sib, rows, cols):
    dma = pltpu.SemaphoreType.DMA
    return pl.pallas_call(
        backward_kernel,
        out_shape=[jax.ShapeDtypeStruct((OBS, C), bf16)] + HALO_OUT,
        in_specs=[vmem()] * 5,
        out_specs=[vmem()] * 4,
        scratch_shapes=[
            VMEM((SLOTS, C), bf16),
            VMEM((OBS, C), bf16),
            VMEM((OBS, C), bf16),
            dma((1,)),
            dma((1,)),
            dma((1,)),
            dma((1,)),
            dma((1,)),
            dma((8,)),
            dma((8,)),
        ],
        compiler_params=pltpu.CompilerParams(
            collective_id=1, has_side_effects=True, vmem_limit_bytes=40 << 20
        ),
    )(grads, route, route_sib, rows, cols)


def sum_kernel(
    parts,
    result,
    to_sib,
    from_sib,
    chip_sum,
    gather,
    owned,
    local_sem,
    sib_send,
    sib_recv,
    data_send,
    data_recv,
    share_send,
    share_recv,
):
    place = Place()
    core, me = place.core, place.chip
    mine = pl.ds(pl.multiple_of(core * HALF_ROWS, 16), HALF_ROWS)
    other = pl.ds(pl.multiple_of((1 - core) * HALF_ROWS, 16), HALF_ROWS)
    barrier, count = greet(place, False)
    to_sib[...] = parts[other, :].astype(bf16)
    pl.semaphore_wait(barrier, count)
    swap = remote(to_sib, from_sib, sib_send.at[0], sib_recv.at[0], place.sibling)
    swap.start()
    swap.wait()
    chip_sum[...] = (parts[mine, :] + from_sib[...].astype(f32)).astype(bf16)

    def block(ref, chip):
        return ref.at[pl.ds(pl.multiple_of(chip * 16, 16), 16)]

    @pl.when(me < HALF)
    def _():
        pltpu.make_async_copy(block(chip_sum, me), gather.at[me], local_sem.at[0]).start()

    def send(step, carry):
        chip, device = place.peer(step)

        @pl.when(chip < HALF)
        def _():
            remote(
                block(chip_sum, chip), gather.at[me], data_send.at[0], data_recv.at[0], device
            ).start()

        return carry

    lax.fori_loop(1, CHIPS, send, 0)
    base = core * HALF_ROWS

    def final(chip):
        return result.at[pl.ds(pl.multiple_of(base + chip * 16, 16), 16)]

    @pl.when(me < HALF)
    def _():
        pltpu.make_async_copy(block(chip_sum, me), gather.at[me], local_sem.at[0]).wait()
        some = pl.ds(0, CHIPS - 1)
        remote(gather.at[some], gather.at[some], data_send.at[0], data_recv.at[0], place.sibling).wait_recv()
        total = jnp.sum(gather[...].astype(f32), axis=0)
        owned[...] = total.astype(bf16)
        pltpu.make_async_copy(owned, final(me), local_sem.at[1]).start()

        def share(step, carry):
            _, device = place.peer(step)
            remote(owned, final(me), share_send.at[0], share_recv.at[0], device).start()
            return carry

        lax.fori_loop(1, CHIPS, share, 0)
        pltpu.make_async_copy(owned, final(me), local_sem.at[1]).wait()
        remote(gather.at[some], gather.at[some], share_send.at[0], share_recv.at[0], place.sibling).wait_send()
        few = pl.ds(0, (HALF - 1) * 16)
        remote(chip_sum.at[few], chip_sum.at[few], data_send.at[0], share_recv.at[0], place.sibling).wait_recv()
        remote(chip_sum.at[few], chip_sum.at[few], data_send.at[0], share_recv.at[0], place.sibling).wait_send()

    @pl.when(me >= HALF)
    def _():
        remote(chip_sum, chip_sum, data_send.at[0], share_recv.at[0], place.sibling).wait_recv()
        remote(chip_sum, chip_sum, data_send.at[0], share_recv.at[0], place.sibling).wait_send()

    last = remote(result.at[mine], result.at[mine], sib_send.at[1], sib_recv.at[1], place.sibling)
    last.start()
    last.wait()


def sum_everywhere(parts):
    dma = pltpu.SemaphoreType.DMA
    return pl.pallas_call(
        sum_kernel,
        out_shape=jax.ShapeDtypeStruct((ROWS, C), bf16),
        in_specs=[vmem()],
        out_specs=vmem(),
        scratch_shapes=[
            VMEM((HALF_ROWS, C), bf16),
            VMEM((HALF_ROWS, C), bf16),
            VMEM((HALF_ROWS, C), bf16),
            VMEM((CHIPS, 16, C), bf16),
            VMEM((16, C), bf16),
            dma((2,)),
            dma((2,)),
            dma((2,)),
            dma((1,)),
            dma((1,)),
            dma((1,)),
            dma((1,)),
        ],
        compiler_params=pltpu.CompilerParams(
            collective_id=2, has_side_effects=True, vmem_limit_bytes=40 << 20
        ),
    )(parts)


def edges(field):
    rows = jnp.stack([field[0], field[CLAT - 1]])
    cols = jnp.stack([field[:, 0], field[:, CLON - 1]])
    return rows, cols


def joined(field, rows, cols, diag):
    north = jnp.concatenate([diag[0, CLAT - 1 :], rows[0], diag[1, CLAT - 1 :]], axis=0)
    south = jnp.concatenate([diag[2, :1], rows[1], diag[3, :1]], axis=0)
    middle = jnp.concatenate([cols[0][:, None], field, cols[1][:, None]], axis=1)
    return jnp.concatenate([north[None], middle, south[None]], axis=0).astype(f32)


def on_device(spectra, owner, cell, w_in, w_out, w_point, w_depth, cotangent):
    cot_rows = cotangent.reshape(CELLS, C)
    target = owner[:, 0]
    zero = jnp.zeros((13, OBS), bf16)
    rows = jnp.concatenate(
        [jnp.stack([target, cell // 16, cell % 16]).astype(bf16), zero], axis=0
    )
    preact, hidden, emb, route = encode(spectra.T, rows, w_in, w_out)
    g_mixed = dot(cot_rows, w_point, ((1,), (1,))).astype(bf16).reshape(CLAT, CLON, C)
    arrived, marks, route_sib, g_rows, g_cols, g_diag = forward_exchange(emb, route, *edges(g_mixed))
    high, low, valid = (marks[:, :, i * CAP : (i + 1) * CAP] for i in range(3))
    places = (high * 16.0 + low + valid - 1.0).astype(i32).reshape(SLOTS)
    one_hot = (places[None, :] == jnp.arange(CELLS, dtype=i32)[:, None]).astype(bf16)
    grid_rows = jnp.dot(one_hot, arrived, preferred_element_type=f32).astype(bf16)
    grid = grid_rows.reshape(CLAT, CLON, C)
    padded_g = joined(g_mixed, g_rows, g_cols, g_diag)
    g_grid = cotangent.astype(f32)
    for k, (a, b) in enumerate(offsets):
        g_grid = g_grid + w_depth[k] * padded_g[1 - a : 1 - a + CLAT, 1 - b : 1 - b + CLON]
    g_grid = g_grid.astype(bf16).reshape(CELLS, C)
    g_arrived = dot(one_hot, g_grid, ((0,), (0,))).astype(bf16)
    g_embedded, x_rows, x_cols, x_diag = backward_exchange(g_arrived, route, route_sib, *edges(grid))
    padded = joined(grid, x_rows, x_cols, x_diag)
    mixed = jnp.zeros((CLAT, CLON, C), f32)
    for k, (a, b) in enumerate(offsets):
        mixed = mixed + w_depth[k] * padded[1 + a : 1 + a + CLAT, 1 + b : 1 + b + CLON]
    mixed_rows = mixed.astype(bf16).reshape(CELLS, C)
    latent = grid_rows.astype(f32) + jnp.dot(mixed_rows, w_point, preferred_element_type=f32)
    latent = latent.astype(bf16).reshape(CLAT, CLON, C)
    grad_point = dot(mixed_rows, cot_rows, ((0,), (0,)))
    g_mixed_f = g_mixed.astype(f32)
    grad_depth = jnp.stack(
        [
            jnp.sum(g_mixed_f * padded[1 + a : 1 + a + CLAT, 1 + b : 1 + b + CLON], axis=(0, 1))
            for a, b in offsets
        ]
    )
    grad_out = dot(hidden, g_embedded, ((0,), (0,)))
    g_hidden = dot(g_embedded, w_out, ((1,), (1,)))
    sig = jax.nn.sigmoid(preact)
    g_preact = (g_hidden * sig * (1.0 + preact * (1.0 - sig))).astype(bf16)
    grad_in = dot(spectra, g_preact, ((0,), (0,)))
    parts = jnp.concatenate(
        [
            grad_in,
            jnp.zeros((ROWS_IN - SPEC, C), f32),
            grad_out,
            grad_point,
            grad_depth,
            jnp.zeros((7, C), f32),
        ],
        axis=0,
    )
    total = sum_everywhere(parts).astype(f32)
    tiles = N_LAT * N_LON
    obs_scale = 1.0 / jnp.sqrt(f32(OBS * tiles))
    cell_scale = 1.0 / jnp.sqrt(f32(CELLS * tiles))
    at = ROWS_IN
    return (
        latent,
        total[:SPEC] * obs_scale,
        total[at : at + C] * obs_scale,
        total[at + C : at + 2 * C] * cell_scale,
        total[at + 2 * C : at + 2 * C + 9] * cell_scale,
    )


def solution(mesh):
    in_specs = (
        P(("lat", "lon"), None),
        P(("lat", "lon"), None),
        P(("lat", "lon")),
        P(),
        P(),
        P(),
        P(),
        P("lat", "lon", None),
    )
    out_specs = (P("lat", "lon", None), P(), P(), P(), P())
    return jax.shard_map(
        on_device, mesh=mesh, in_specs=in_specs, out_specs=out_specs, check_vma=False
    )
```

time: 321 us -> 162 us (0.50)
  waiting for transfers between devices: 113 us -> 0 us
  Pallas kernels: 0 us -> 98.8 us
  blocking collectives: 67.8 us -> 0 us
  starting transfers between devices: 49 us -> 0 us
  matrix products: 33 us -> 19.2 us
  between operations: 14.4 us -> 1.08 us
  other arithmetic: 33.3 us -> 24.1 us
  local copies, waits for them, and re-layouts: 10.5 us -> 18.2 us
    pallas_call x0 -> x4, Pallas kernels: none -> 98.8 us  [the longest x1 41 us: sum_everywhere(): pl.pallas_call(sum_kernel, out_shape=jax.ShapeDtypeStruct((ROWS, C), bf16...]
    psum x1 -> x0, waiting for transfers between devices: 82.1 us -> none  [on_device(): lax.psum((grad_in, grad_out, grad_point, grad_depth), ('lat', 'lon'))]
    psum x1 -> x0, blocking collectives: 67.8 us -> none  [on_device(): lax.psum((grad_in, grad_out, grad_point, grad_depth), ('lat', 'lon'))]
    all_to_all x3 -> x0, starting transfers between devices: 27.2 us -> none  [the longest x1 11.5 us: send_out(): lax.all_to_all(places.reshape(tiles, cap), ('lat', 'lon'), split_axis=0,...]
    ppermute x8 -> x0, starting transfers between devices: 21.5 us -> none  [the longest x4 13.3 us: extended(): lax.ppermute(lax.slice_in_dim(block, 0, width, axis=dim), axis, backward)]
    all_to_all x3 -> x0, waiting for transfers between devices: 19.3 us -> none  [the longest x1 17.4 us: send_out(): lax.all_to_all(values.reshape(tiles, cap, width), ('lat', 'lon'), split_a...]
    dot_general x9 -> x7, matrix products: 33 us -> 19.2 us  [the longest x5 12.9 us: dot(): return lax.dot_general(a, b, (dims, ((), ())), preferred_element_type=f32)]
    ppermute x8 -> x0, waiting for transfers between devices: 11.2 us -> none  [the longest x4 8.63 us: extended(): lax.ppermute(lax.slice_in_dim(block, 0, width, axis=dim), axis, backward)]
  transfers between devices with their start and end apart: 12 -> 0, of which waited for: 7 -> 0; matrix products, arithmetic and copies ran while one was open for 11% -> 0% of each run, Pallas kernels for 0% -> 0%
where the time goes in v1:
time: 162 us; the launch traced here: 161 us
  Pallas kernels  98.8 us (61%)
  other arithmetic  24.1 us (15%)
  matrix products  19.2 us (12%)
  local copies, waits for them, and re-layouts  18.2 us (11%)
    pallas_call x1, Pallas kernels, sum_everywhere(): pl.pallas_call(sum_kernel, out_shape=jax.ShapeDtypeStruct((ROWS, C), bf16...  41 us
    pallas_call x1, Pallas kernels, forward_exchange(): pl.pallas_call(forward_kernel, out_shape=[jax.ShapeDtypeStruct((SLOTS, C)...  30.1 us
    pallas_call x1, Pallas kernels, backward_exchange(): pl.pallas_call(backward_kernel, out_shape=[jax.ShapeDtypeStruct((OBS, C),...  25.9 us
    dot_general x5, matrix products, dot(): return lax.dot_general(a, b, (dims, ((), ())), preferred_element_type=f32)  12.9 us
    concatenate x1, local copies, waits for them, and re-layouts, on_device(): jnp.concatenate([grad_in, jnp.zeros((ROWS_IN - SPEC, C), f32), grad_out,...  9.1 us
    unnamed x32, local copies, waits for them, and re-layouts  7.46 us
    convert_element_type x1, other arithmetic, on_device(): g_grid = g_grid.astype(bf16).reshape(CELLS, C)  6.37 us
    reduce_sum x1, other arithmetic, on_device(): jnp.sum(g_mixed_f * padded[1 + a:1 + a + CLAT, 1 + b:1 + b + CLON], axis=...  5.17 us

profile of v1, /device:TPU:1, one launch (start us, length us, event | category | flops | bytes accessed | tf_op | source)
XLA Modules:
  0.0 161.4 jit_solution(5270245297855035703)
XLA Ops:
  0.6 0.7 convert_bitcast_fusion
  1.4 0.7 fusion.40
  2.1 1.1 fusion.46
  3.3 3.0 %convolution_convert_fusion = bf16[2048,512]{1,0:T(8,128)(2,1)S(1)} fusion(bf16[2048,512]{1,0:T(8,128)(2,1)} %bitcast.116, bf16[512,512]{1,0:T(8,128)(2,1)S(1)} %copy-done), kind=kOutput, calls=%fused_computation.44 | convolution fusion | flops 1074790400 | bytes 4718592 | tf_op jit(solution)/shard_map/dot_general | solution.py:38
  6.5 1.2 copy-done.7
  7.7 1.8 %shard_map.119 = (f32[512,512]{1,0:T(8,128)S(1)}, bf16[512,512]{1,0:T(8,128)(2,1)S(1)}, bf16[512,640]{1,0:T(8,128)(2,1)S(1)}, s32[8,512]{1,0:T(8,128)S(1)}) custom-call(bf16[616,512]{1,0:T(8,128)(2,1)S(1)} %bitcast.111, bf16[16,512]{1,0:T(8,128)(2,1)S(1)} %fusion.39.rows, bf16[616,512]{1,0:T(8,128)(2,1)S(1)} %copy-done.2, bf16[512,512]{1,0:T(8,128)(2,1)S(1)} %copy-done.4), custom_call_target="tpu_custom_call" | custom-call | tf_op jit(solution)/shard_map/pallas_call | solution.py:199
  9.5 1.0 copy-done.5
  10.5 30.1 %shard_map.120 = (bf16[1024,512]{1,0:T(8,128)(2,1)S(1)}, f32[64,2,128]{2,1,0:T(2,128)S(1)}, s32[8,512]{1,0:T(8,128)S(1)}, bf16[2,128,512]{2,1,0:T(8,128)(2,1)S(1...) custom-call(bf16[512,640]{1,0:T(8,128)(2,1)S(1)} %get-tuple-element.19.emb, ...), custom_call_target="tpu_custom_call" | custom-call | tf_op jit(solution)/shard_map/pallas_call | solution.py:338
  40.6 1.0 copy-done.6
  41.5 0.2 add_convert_fusion.2
  41.8 0.1 eq.17
  42.1 3.7 %fusion.23 = bf16[2048,512]{1,0:T(8,128)(2,1)S(1)} fusion(bf16[1024,512]{1,0:T(8,128)(2,1)} %copy-done.6, s32[1024]{0:T(1024)S(1)} %eq.17), kind=kOutput, calls=%fused_computation.45 | convolution fusion | flops 2150629376 | bytes 3149824 | tf_op jit(solution)/shard_map/dot_general | solution.py:601
  46.0 1.2 copy-done.10
  47.2 0.9 maximum_convert_fusion
  48.2 6.4 %fusion.12 = bf16[16,128,512]{2,1,0:T(8,128)(2,1)} fusion(f32[18,130,512]{2,1,0:T(8,128)S(1)} %maximum_convert_fusion, bf16[16,128,512]{2,1,0:T(8,128)(2,1)S(1)} %copy-done.12, f32[512]{0:T(512)S(1)} %bitcast.135, f32[512]{0:T(512)S(1)} %bitcast.137, f32[512]{0:T(512)S(1)} %bitcast.123, f32[512]{0:T(512)S(1)} %bitcast.125, f32[512]{0:T(512)S(1)} %bitcast.127, ...), kind=kLoop, calls=%fused_computation.23 | loop fusion | flops 20971520 | bytes 41961472 | tf_op jit(solution)/shard_map/convert_element_type | solution.py:607
  54.6 4.0 %fusion.24.grads = bf16[1024,512]{1,0:T(8,128)(2,1)S(1)} fusion(bf16[2048,512]{1,0:T(8,128)(2,1)} %bitcast.118, s32[1024]{0:T(1024)S(1)} %eq.17), kind=kOutput, calls=%fused_computation.48 | convolution fusion | flops 2150105088 | bytes 3149824 | tf_op jit(solution)/shard_map/dot_general | solution.py:38
  58.6 25.9 %shard_map.121 = (bf16[512,512]{1,0:T(8,128)(2,1)S(1)}, bf16[2,128,512]{2,1,0:T(8,128)(2,1)S(1)}, bf16[2,16,512]{2,1,0:T(8,128)(2,1)S(1)}, bf16[4,16,512]{2,1,0:T(8,128)(2,1)S(1)}) custom-call(bf16[1024,512]{1,0:T(8,128)(2,1)S(1)} %fusion.24.grads, s32[8,512]{1,0:T(8,128)S(1)} %get-tuple-element.20.route, s32[8,512]{1,0:T(8,128)S(1)} %get-tuple-element.26.route_sib, ...), custom_call_target="tpu_custom_call" | custom-call | tf_op jit(solution)/shard_map/pallas_call | solution.py:442
  84.6 3.3 %convolution_bitcast_fusion = f32[616,512]{1,0:T(8,128)} fusion(bf16[512,616]{0,1:T(8,128)(2,1)S(1)} %copy-done.3, bf16[512,512]{1,0:T(8,128)(2,1)S(1)} %get-tuple-element.30, bf16[512,512]{1,0:T(8,128)(2,1)S(1)} %copy-done.4, f32[512,512]{1,0:T(8,128)} %copy-done.5), kind=kOutput, calls=%fused_computation.49 | convolution fusion | flops 593756160 | bytes 3989504 | tf_op jit(solution)/shard_map/dot_general | solution.py:38
  87.9 0.5 fusion.47
  88.5 1.0 copy-done.11
  89.5 0.9 maximum_convert_fusion.1
  90.3 5.2 %fusion.10 = (f32[512]{0:T(512)S(1)}, f32[512]{0:T(512)S(1)}, f32[512]{0:T(512)S(1)}, f32[512]{0:T(512)S(1)}, f32[512]{0:T(512)S(1)}, /*index=5*/f32[512]{0:T(51...) fusion(f32[18,130,512]{2,1,0:T(8,128)S(1)} %maximum_convert_fusion.1, bf16[2048,512]{1,0:T(8,128)(2,1)S(1)} %copy-done.9), kind=kLoop, calls=%fused_computation.20 | loop fusion | flops 19918336 | bytes 39864320 | tf_op jit(solution)/shard_map/reduce_sum | solution.py:621
  95.5 5.1 %add_convert_fusion.1 = bf16[16,128,512]{2,1,0:T(8,128)(2,1)S(1)} fusion(f32[18,130,512]{2,1,0:T(8,128)S(1)} %maximum_convert_fusion.1, f32[512]{0:T(512)S(1)} %bitcast.136, f32[512]{0:T(512)S(1)} %bitcast.138, f32[512]{0:T(512)S(1)} %bitcast.124, f32[512]{0:T(512)S(1)} %bitcast.126, f32[512]{0:T(512)S(1)} %bitcast.128, f32[512]{0:T(512)S(1)} %bitcast.130, ...), kind=kLoop, calls=%fused_computation.41 | loop fusion | flops 18874368 | bytes 39864320 | tf_op jit(solution)/shard_map/convert_element_type | solution.py:614
  100.7 2.6 %add_convert_fusion = bf16[2048,512]{1,0:T(8,128)(2,1)} fusion(bf16[2048,512]{1,0:T(8,128)(2,1)S(1)} %copy-done.11, bf16[2048,512]{1,0:T(8,128)(2,1)S(1)} %bitcast.117, bf16[512,512]{1,0:T(8,128)(2,1)S(1)} %copy-done), kind=kOutput, calls=%fused_computation.40 | convolution fusion | flops 1076887552 | bytes 6815744 | tf_op jit(solution)/shard_map/dot_general | solution.py:615
  103.3 2.2 %convolution_bitcast_fusion.1 = f32[512,512]{1,0:T(8,128)} fusion(bf16[16,128,512]{2,1,0:T(8,128)(2,1)S(1)} %add_convert_fusion.1, bf16[16,128,512]{2,1,0:T(8,128)(2,1)S(1)} %copy-done.13), kind=kOutput, calls=%fused_computation.50 | convolution fusion | flops 1073741824 | bytes 5242880 | tf_op jit(solution)/shard_map/dot_general | solution.py:38
  105.5 9.1 %concatenate.39.parts = f32[1664,512]{1,0:T(8,128)} concatenate(f32[616,512]{1,0:T(8,128)S(1)} %copy-done.14, f32[8,512]{1,0:T(8,128)S(1)} %broadcast_in_dim.24, f32[512,512]{1,0:T(8,128)S(1)} %fusion.47, f32[512,512]{1,0:T(8,128)} %convolution_bitcast_fusion.1, f32[1,512]{1,0:T(1,128)S(1)} %bitcast.147, f32[1,512]{1,0:T(1,128)S(1)} %bitcast.146, f32[1,512]{1,0:T(1,128)S(1)} %bitcast.145, ...), dimensions={0} | concatenate | bytes 6815744 | tf_op jit(solution)/shard_map/concatenate | solution.py:630
  114.6 2.0 %copy-done.1 = f32[1664,512]{1,0:T(8,128)S(1)} copy-done((f32[1664,512]{1,0:T(8,128)S(1)}, f32[1664,512]{1,0:T(8,128)}, u32[]{:S(2)}) %copy-start.1) | copy-done | bytes 3407896
  116.6 41.0 %shard_map.122 = bf16[1664,512]{1,0:T(8,128)(2,1)S(1)} custom-call(f32[1664,512]{1,0:T(8,128)S(1)} %copy-done.1), custom_call_target="tpu_custom_call" | custom-call | tf_op jit(solution)/shard_map/pallas_call | solution.py:550
  157.5 0.5 convert_element_type.57
  158.0 0.6 slice_multiply_fusion.12
  158.6 1.2 slice_multiply_fusion.9
  159.8 1.5 slice_multiply_fusion.10
  (54 shorter events, 0.8 us)
Async XLA Ops:
  0.6 2.6 %copy-start = (bf16[512,512]{1,0:T(8,128)(2,1)S(1)}, bf16[512,512]{1,0:T(8,128)(2,1)}, u32[]{:S(2)}) copy-start(bf16[512,512]{1,0:T(8,128)(2,1)} %param.13) | copy-start | bytes 1572868
  3.3 4.4 %copy-start.2 = (bf16[616,512]{1,0:T(8,128)(2,1)S(1)}, bf16[616,512]{1,0:T(8,128)(2,1)}, u32[]{:S(2)}) copy-start(bf16[616,512]{1,0:T(8,128)(2,1)} %w_in.1) | copy-start | bytes 1892356
  3.3 4.4 %copy-start.3 = (bf16[512,616]{0,1:T(8,128)(2,1)S(1)}, bf16[512,616]{0,1:T(8,128)(2,1)}, u32[]{:S(2)}) copy-start(bf16[512,616]{0,1:T(8,128)(2,1)} %param.8) | copy-start | bytes 1892356
  3.3 4.4 %copy-start.4 = (bf16[512,512]{1,0:T(8,128)(2,1)S(1)}, bf16[512,512]{1,0:T(8,128)(2,1)}, u32[]{:S(2)}) copy-start(bf16[512,512]{1,0:T(8,128)(2,1)} %w_out.1) | copy-start | bytes 1572868
  6.3 1.4 copy-start.7
  9.5 1.0 copy-start.5
  40.6 1.0 copy-start.6
  42.1 5.1 %copy-start.8 = (bf16[2048,512]{1,0:T(8,128)(2,1)S(1)}, bf16[2048,512]{1,0:T(8,128)(2,1)}, u32[]{:S(2)}) copy-start(bf16[2048,512]{1,0:T(8,128)(2,1)} %copy-done.7) | copy-start | bytes 6291460
  45.9 1.3 copy-start.10
  46.0 2.2 %copy-start.12 = (bf16[16,128,512]{2,1,0:T(8,128)(2,1)S(1)}, bf16[16,128,512]{2,1,0:T(8,128)(2,1)}, u32[]{:S(2)}) copy-start(bf16[16,128,512]{2,1,0:T(8,128)(2,1)} %param.15) | copy-start | bytes 6291460
  87.9 1.6 copy-start.11
  88.3 2.0 %copy-start.9 = (bf16[2048,512]{1,0:T(8,128)(2,1)S(1)}, bf16[2048,512]{1,0:T(8,128)(2,1)}, u32[]{:S(2)}) copy-start(bf16[2048,512]{1,0:T(8,128)(2,1)} %copy-done.7) | copy-start | bytes 6291460
  100.6 2.6 %copy-start.13 = (bf16[16,128,512]{2,1,0:T(8,128)(2,1)S(1)}, bf16[16,128,512]{2,1,0:T(8,128)(2,1)}, u32[]{:S(2)}) copy-start(bf16[16,128,512]{2,1,0:T(8,128)(2,1)} %param.15) | copy-start | bytes 6291460
  103.3 2.3 %copy-start.14 = (f32[616,512]{1,0:T(8,128)S(1)}, f32[616,512]{1,0:T(8,128)}, u32[]{:S(2)}) copy-start(f32[616,512]{1,0:T(8,128)} %convolution_bitcast_fusion) | copy-start | bytes 3784708
  114.6 2.0 %copy-start.1 = (f32[1664,512]{1,0:T(8,128)S(1)}, f32[1664,512]{1,0:T(8,128)}, u32[]{:S(2)}) copy-start(f32[1664,512]{1,0:T(8,128)} %concatenate.39.parts) | copy-start | bytes 10223620

commit v2 on v0

v2 whole, which is shorter than its diff:
```python
import functools

import jax
import jax.numpy as jnp
from jax import lax
from jax.experimental import pallas as pl
from jax.experimental.pallas import tpu as pltpu
from jax.sharding import PartitionSpec as P

offsets = [(a, b) for a in (-1, 0, 1) for b in (-1, 0, 1)]
f32, bf16, i32 = jnp.float32, jnp.bfloat16, jnp.int32

N_LAT, N_LON, SIDE = 8, 16, 4
CHIPS = N_LAT // 2 * N_LON
CAP = 8
SLOT = 2 * CAP
SLOTS = CHIPS * SLOT
OBS = 512
C = 512
CLAT, CLON = 16, 128
CELLS = CLAT * CLON
SPEC = 616
META = 128
ROWS_IN = 624
PART = 256
CHUNK = 128

VMEM = pltpu.VMEM


def vmem():
    return pl.BlockSpec(memory_space=pltpu.VMEM)


def dot(a, b, dims):
    return lax.dot_general(a, b, (dims, ((), ())), preferred_element_type=f32)


class Place:
    def __init__(self):
        self.lat = lax.axis_index("lat")
        self.lon = lax.axis_index("lon")
        self.core = self.lat % 2
        self.x = self.lat // 2
        self.chip = self.x * N_LON + self.lon
        self.sibling = (self.x * 2 + 1 - self.core, self.lon)

    def peer(self, step):
        step = (step * 37) % CHIPS
        x = (self.x + step // N_LON) % (N_LAT // 2)
        z = (self.lon // SIDE + step // SIDE) % SIDE
        y = (self.lon + step) % SIDE
        lon = z * SIDE + y
        return x * N_LON + lon, (x * 2 + self.core, lon)

    def of_chip(self, chip):
        return (chip // N_LON * 2 + self.core, chip % N_LON)


def remote(src, dst, send, recv, device):
    return pltpu.make_async_remote_copy(
        src_ref=src,
        dst_ref=dst,
        send_sem=send,
        recv_sem=recv,
        device_id=device,
        device_id_type=pl.DeviceIdType.MESH,
    )


def greet(place, halo):
    barrier = pltpu.get_barrier_semaphore()

    def hello(device):
        pl.semaphore_signal(
            barrier, inc=1, device_id=device, device_id_type=pl.DeviceIdType.MESH
        )

    def one(step, carry):
        hello(place.peer(step)[1])
        return carry

    lax.fori_loop(1, CHIPS, one, 0)
    if not halo:
        hello(place.sibling)
        return barrier, CHIPS
    for side in (-1, 1):
        inside = (place.lat + side >= 0) & (place.lat + side < N_LAT)

        @pl.when(inside)
        def _(side=side):
            for turn in (-1, 0, 1):
                hello((place.lat + side, (place.lon + turn + N_LON) % N_LON))

    edges = (place.lat > 0).astype(i32) + (place.lat < N_LAT - 1).astype(i32)
    return barrier, CHIPS - 1 + 3 * edges


class Halo:
    def __init__(self, place, ext, cols, to_cols, to_diag, send, recv):
        self.place = place
        self.ext, self.to_diag = ext, to_diag
        lat, lon = place.lat, place.lon
        east, west = (lon + 1) % N_LON, (lon + N_LON - 1) % N_LON
        has_north, has_south = lat > 0, lat < N_LAT - 1
        south, north = jnp.minimum(lat + 1, N_LAT - 1), jnp.maximum(lat - 1, 0)
        plan = [
            (ext.at[CLAT], ext.at[0], (south, lon), has_south, has_north),
            (ext.at[1], ext.at[CLAT + 1], (north, lon), has_north, has_south),
            (cols.at[1], to_cols.at[0], (lat, east), None, None),
            (cols.at[0], to_cols.at[1], (lat, west), None, None),
            (cols.at[1], to_diag.at[0], (south, east), has_south, has_north),
            (cols.at[0], to_diag.at[1], (south, west), has_south, has_north),
            (cols.at[1], to_diag.at[2], (north, east), has_north, has_south),
            (cols.at[0], to_diag.at[3], (north, west), has_north, has_south),
        ]
        self.plan = [
            (remote(src, dst, send.at[i], recv.at[i], device), sends, receives)
            for i, (src, dst, device, sends, receives) in enumerate(plan)
        ]

    def start(self):
        for copy, sends, _ in self.plan:
            if sends is None:
                copy.start()
            else:
                pl.when(sends)(copy.start)

    def wait(self):
        for copy, sends, receives in self.plan:
            if sends is None:
                copy.wait_send()
                copy.wait_recv()
            else:
                pl.when(sends)(copy.wait_send)
                pl.when(receives)(copy.wait_recv)

    def clear_outside(self):
        @pl.when(self.place.lat == 0)
        def _():
            self.ext[0] = jnp.zeros((CLON, C), bf16)
            self.to_diag[0] = jnp.zeros((CLAT, C), bf16)
            self.to_diag[1] = jnp.zeros((CLAT, C), bf16)

        @pl.when(self.place.lat == N_LAT - 1)
        def _():
            self.ext[CLAT + 1] = jnp.zeros((CLON, C), bf16)
            self.to_diag[2] = jnp.zeros((CLAT, C), bf16)
            self.to_diag[3] = jnp.zeros((CLAT, C), bf16)


def vector_encode(spec_t, rows, w_in, w_out, preact, hidden, emb, route):
    pre = dot(spec_t[...], w_in[...], ((0,), (0,)))
    preact[...] = pre
    hid = (pre * (1.0 / (1.0 + jnp.exp(-pre)))).astype(bf16)
    hidden[...] = hid
    emb[:, :C] = dot(hid, w_out[...], ((1,), (0,))).astype(bf16)
    values = rows[...]
    down = lax.broadcasted_iota(i32, (OBS, OBS), 0)
    across = lax.broadcasted_iota(i32, (OBS, OBS), 1)
    eye = (down == across).astype(f32).astype(bf16)
    columns = dot(eye, values, ((1,), (1,)))
    tile_col, high_col, low_col = columns[:, 0:1], columns[:, 1:2], columns[:, 2:3]
    tile_row = values[0:1, :].astype(f32)
    tiles = N_LAT * N_LON
    hits = (tile_col == lax.broadcasted_iota(i32, (OBS, tiles), 1).astype(f32)).astype(f32)
    lower = (across <= down).astype(f32).astype(bf16)
    count = dot(lower, hits.astype(bf16), ((1,), (0,)))
    pos_col = (jnp.sum(count * hits, axis=1, keepdims=True) - 1.0).astype(i32)
    hits_t = (tile_row == lax.broadcasted_iota(i32, (tiles, OBS), 0).astype(f32)).astype(f32)
    upper = (down <= across).astype(f32).astype(bf16)
    count_t = dot(hits_t.astype(bf16), upper, ((1,), (0,)))
    pos_row = (jnp.sum(count_t * hits_t, axis=0, keepdims=True) - 1.0).astype(i32)
    lane = lax.broadcasted_iota(i32, (OBS, META), 1)
    kind = lane // CAP
    value = jnp.where(kind == 0, high_col, jnp.where(kind == 1, low_col, 1.0))
    keep = (lane % CAP == pos_col) & (kind < 3)
    emb[:, C:] = jnp.where(keep, value, 0.0).astype(bf16)
    tile = tile_row.astype(i32)
    lat, lon = tile // N_LON, tile % N_LON
    chip = lat // 2 * N_LON + lon
    route[...] = jnp.concatenate(
        [chip * SLOT + pos_row, lat % 2, chip, jnp.zeros((5, OBS), i32)], axis=0
    )


def slot_keys(route, mine, core):
    return jnp.where(route[1:2, :] == mine, route[0:1, :] + CAP * core, -1)


class Round:
    def __init__(self, first, count, owner):
        self.first, self.count, self.owner = first, count, owner
        self.half = count * 16


EARLY = Round(0, 36, 0)
LATE = Round(1152, 17, 36)
PARTS = 1152 + 544

SIB_EMB, SIB_ROUTE, MARK, DATA, BACK, SIB_PART = range(6)
ROUND_SEMS = ((6, 7, 8, 9), (10, 11, 12, 13))
SEMS = 14


def block(ref, chip, size=SLOT):
    return ref.at[pl.ds(pl.multiple_of(chip * size, size), size)]


def edge_columns(ext, cols):
    for side, (at, row) in enumerate(((0, 0), (CLON - 16, 15))):
        for i in range(CLAT):
            cols[side, i : i + 1, :] = ext[1 + i, at : at + 16, :].astype(f32)[row : row + 1]


def side_columns(to_cols, to_diag, west, east):
    for side, (into, above, below) in enumerate(((west, 0, 2), (east, 1, 3))):
        into[0:1, :] = to_diag[above].astype(f32)[CLAT - 1 : CLAT]
        into[1 : CLAT + 1, :] = to_cols[side].astype(f32)
        into[CLAT + 1 : CLAT + 2, :] = to_diag[below].astype(f32)[0:1]


def side_sums(west, east, weight, sides):
    for side, ref in ((0, west), (1, east)):
        b = 2 * side
        total = (
            weight(b) * ref[0:CLAT, :]
            + weight(3 + b) * ref[1 : CLAT + 1, :]
            + weight(6 + b) * ref[2 : CLAT + 2, :]
        )
        for i in range(CLAT):
            sides[side, i, 0:1, :] = total[i : i + 1, :]


def conv_part(rows, sides, i, lanes, weight):
    columns = [
        weight(b) * rows[0] + weight(3 + b) * rows[1] + weight(6 + b) * rows[2] for b in range(3)
    ]
    index = lax.broadcasted_iota(i32, (CLON, CHUNK), 0)
    left = jnp.where(index == 0, sides[0, i, 0:1, lanes], pltpu.roll(columns[0], 1, 0))
    right = jnp.where(
        index == CLON - 1, sides[1, i, 0:1, lanes], pltpu.roll(columns[2], CLON - 1, 0)
    )
    return columns[1] + left + right


def kernel(
    spec_in,
    rows,
    w_in_in,
    w_out_in,
    w_point_in,
    w_depth,
    cot_in,
    latent,
    result,
    spec_t,
    w_in,
    w_out,
    w_point,
    cot,
    preact,
    hidden,
    emb,
    emb_sib,
    route,
    route_sib,
    outgoing,
    arrived,
    marks,
    places,
    gm_ext,
    grid_ext,
    cols_f,
    cols,
    to_cols,
    to_diag,
    cols_x,
    to_cols_x,
    to_diag_x,
    west,
    east,
    sides,
    g_grid,
    g_arrived,
    returned,
    part,
    part_sib,
    g_emb,
    mixed,
    parts,
    swap_out,
    swap_in,
    chip_sum,
    gather,
    owned,
    load_sem,
    local_sem,
    send_sem,
    recv_sem,
    halo_send,
    halo_recv,
):
    place = Place()
    core, me = place.core, place.chip
    loads = [
        pltpu.make_async_copy(src, dst, load_sem.at[i])
        for i, (src, dst) in enumerate(
            (
                (spec_in, spec_t),
                (w_in_in, w_in),
                (w_out_in, w_out),
                (w_point_in, w_point),
                (cot_in, cot),
            )
        )
    ]
    for copy in loads:
        copy.start()
    barrier, count = greet(place, True)

    def cross(src, dst, index, device):
        return remote(src, dst, send_sem.at[index], recv_sem.at[index], device)

    halo_g = Halo(place, gm_ext, cols, to_cols, to_diag, halo_send.at[0], halo_recv.at[0])
    halo_x = Halo(place, grid_ext, cols_x, to_cols_x, to_diag_x, halo_send.at[1], halo_recv.at[1])
    halo_g.clear_outside()
    halo_x.clear_outside()
    for copy in loads[:3]:
        copy.wait()
    vector_encode(spec_t, rows, w_in, w_out, preact, hidden, emb, route)
    for copy in loads[3:]:
        copy.wait()

    def mix_back(i, carry):
        rows4 = cot[pl.ds(pl.multiple_of(i * 512, 512), 512), :]
        gm = dot(rows4, w_point[...], ((1,), (1,))).astype(bf16)
        gm_ext[pl.ds(1 + 4 * i, 4)] = gm.reshape(4, CLON, C)
        return carry

    lax.fori_loop(0, CLAT // 4, mix_back, 0)
    edge_columns(gm_ext, cols_f.at[pl.ds(0, 2)])
    cols[...] = cols_f[0:2].astype(bf16)
    pl.semaphore_wait(barrier, count)

    swaps = [
        cross(emb, emb_sib, SIB_EMB, place.sibling),
        cross(route, route_sib, SIB_ROUTE, place.sibling),
    ]
    for copy in swaps:
        copy.start()
    halo_g.start()

    def spread(key, values, more):
        def one(i, carry):
            at = pl.multiple_of(i * PART, PART)
            index = lax.broadcasted_iota(i32, (PART, OBS), 0) + at
            pick = (index == key).astype(f32).astype(bf16)
            new = dot(pick, values[:, :C], ((1,), (0,)))
            if more:
                new = new + outgoing[pl.ds(at, PART), :].astype(f32)
            outgoing[pl.ds(at, PART), :] = new.astype(bf16)
            return carry

        lax.fori_loop(0, SLOTS // PART, one, 0)

    chips = lax.broadcasted_iota(i32, (CHIPS, OBS), 0)

    def marked(info, values):
        wanted = (info[2:3, :] == chips) & (info[1:2, :] == core)
        return dot(wanted.astype(f32).astype(bf16), values[:, C:], ((1,), (0,)))

    spread(slot_keys(route[...], core, core), emb, False)
    own = marked(route, emb)
    for copy in swaps:
        copy.wait()
    other = marked(route_sib, emb_sib)
    marks[:, 0, :] = jnp.where(core == 0, own, other)
    marks[:, 1, :] = jnp.where(core == 0, other, own)
    spread(slot_keys(route_sib[...], core, 1 - core), emb_sib, True)
    keep = [
        pltpu.make_async_copy(marks.at[me], places.at[me], local_sem.at[0]),
        pltpu.make_async_copy(block(outgoing, me), block(arrived, me), local_sem.at[1]),
    ]
    for copy in keep:
        copy.start()

    def send_marks(step, carry):
        chip, device = place.peer(step)
        cross(marks.at[chip], places.at[me], MARK, device).start()
        return carry

    lax.fori_loop(1, CHIPS, send_marks, 0)

    def send_data(step, carry):
        chip, device = place.peer(step)
        cross(block(outgoing, chip), block(arrived, me), DATA, device).start()
        return carry

    lax.fori_loop(1, CHIPS, send_data, 0)
    some = pl.ds(0, (CHIPS - 1) * SLOT)
    few = pl.ds(0, CHIPS - 1)

    halo_g.wait()
    side_columns(to_cols, to_diag, west, east)
    side_sums(west, east, lambda k: w_depth[8 - k : 9 - k, :], sides)

    def conv_back(i, carry):
        for chunk in range(C // CHUNK):
            lanes = slice(chunk * CHUNK, (chunk + 1) * CHUNK)
            three = [gm_ext[i + a, :, lanes].astype(f32) for a in range(3)]
            acc = conv_part(three, sides, i, lanes, lambda k: w_depth[8 - k : 9 - k, lanes])
            at = pl.ds(pl.multiple_of(i * CLON, CLON), CLON)
            g_grid[at, lanes] = (cot[at, lanes].astype(f32) + acc).astype(bf16)
        return carry

    lax.fori_loop(0, CLAT, conv_back, 0)

    for copy in keep:
        copy.wait()
    all_marks = cross(marks.at[few], places.at[few], MARK, place.sibling)
    all_marks.wait_recv()
    tables = [places[:, k, :].astype(bf16) for k in range(2)]
    down = lax.broadcasted_iota(i32, (SLOTS, CHIPS), 0)
    expand = (down // SLOT == lax.broadcasted_iota(i32, (SLOTS, CHIPS), 1)).astype(f32).astype(bf16)
    slot = lax.broadcasted_iota(i32, (SLOTS, META), 0)
    lane = lax.broadcasted_iota(i32, (SLOTS, META), 1)
    wide = [dot(expand, table, ((1,), (0,))) for table in tables]
    mine = jnp.where((slot // CAP) % 2 == 0, wide[0], wide[1])
    factor = jnp.where(lane < CAP, 16.0, 1.0)
    place_col = (
        jnp.sum(jnp.where(lane % CAP == slot % CAP, mine * factor, 0.0), axis=1, keepdims=True) - 1.0
    ).astype(i32)
    across = lax.broadcasted_iota(i32, (CHIPS, SLOTS), 1)
    expand_t = (across // SLOT == lax.broadcasted_iota(i32, (CHIPS, SLOTS), 0)).astype(f32).astype(bf16)
    slot_t = lax.broadcasted_iota(i32, (META, SLOTS), 1)
    lane_t = lax.broadcasted_iota(i32, (META, SLOTS), 0)
    wide_t = [dot(table, expand_t, ((0,), (0,))) for table in tables]
    mine_t = jnp.where((slot_t // CAP) % 2 == 0, wide_t[0], wide_t[1])
    factor_t = jnp.where(lane_t < CAP, 16.0, 1.0)
    place_row = (
        jnp.sum(jnp.where(lane_t % CAP == slot_t % CAP, mine_t * factor_t, 0.0), axis=0, keepdims=True)
        - 1.0
    ).astype(i32)
    cells = lax.broadcasted_iota(i32, (PART, CELLS), 1)
    for at in range(0, SLOTS, PART):
        pick = (place_col[at : at + PART] == cells).astype(f32).astype(bf16)
        g_arrived[at : at + PART, :] = dot(pick, g_grid[...], ((1,), (0,))).astype(bf16)
    keep_back = pltpu.make_async_copy(block(g_arrived, me), block(returned, me), local_sem.at[2])
    keep_back.start()

    def send_back(step, carry):
        chip, device = place.peer(step)
        cross(block(g_arrived, chip), block(returned, me), BACK, device).start()
        return carry

    lax.fori_loop(1, CHIPS, send_back, 0)

    all_data = cross(outgoing.at[some], arrived.at[some], DATA, place.sibling)
    all_data.wait_recv()

    def bin_rows(i, carry):
        index = lax.broadcasted_iota(i32, (PART, SLOTS), 0) + i * PART
        pick = (index == place_row).astype(f32).astype(bf16)
        cells_here = dot(pick, arrived[...], ((1,), (0,))).astype(bf16)
        grid_ext[pl.ds(1 + 2 * i, 2)] = cells_here.reshape(2, CLON, C)
        return carry

    lax.fori_loop(0, CELLS // PART, bin_rows, 0)
    edge_columns(grid_ext, cols_f.at[pl.ds(2, 2)])
    cols_x[...] = cols_f[2:4].astype(bf16)
    halo_x.start()
    halo_x.wait()
    side_columns(to_cols_x, to_diag_x, west, east)
    side_sums(west, east, lambda k: w_depth[k : k + 1, :], sides)
    depth = LATE.first + C
    for chunk in range(C // CHUNK):
        lanes = slice(chunk * CHUNK, (chunk + 1) * CHUNK)

        def conv_forward(i, sums, lanes=lanes):
            three = [grid_ext[i + a, :, lanes].astype(f32) for a in range(3)]
            acc = conv_part(three, sides, i, lanes, lambda k: w_depth[k : k + 1, lanes])
            at = pl.ds(pl.multiple_of(i * CLON, CLON), CLON)
            mixed[at, lanes] = acc.astype(bf16)
            middle = gm_ext[i + 1, :, lanes].astype(f32)
            index = lax.broadcasted_iota(i32, (CLON, CHUNK), 0)
            shifted = [
                jnp.where(index == CLON - 1, 0.0, pltpu.roll(middle, CLON - 1, 0)),
                middle,
                jnp.where(index == 0, 0.0, pltpu.roll(middle, 1, 0)),
            ]
            return tuple(
                sums[3 * a + b] + jnp.sum((shifted[b] * three[a]).reshape(16, 8, CHUNK), axis=0)
                for a in range(3)
                for b in range(3)
            )

        sums = lax.fori_loop(0, CLAT, conv_forward, tuple(jnp.zeros((8, CHUNK), f32) for _ in range(9)))
        for k, (a, b) in enumerate(offsets):
            total = jnp.sum(sums[k], axis=0, keepdims=True)
            if b:
                side = (west if b < 0 else east)[1 + a : 1 + a + CLAT, lanes]
                edge = cols_f[0 if b < 0 else 1, :, lanes].astype(bf16).astype(f32)
                total = total + jnp.sum(side * edge, axis=0, keepdims=True)
            parts[depth + k : depth + k + 1, lanes] = total
    parts[SPEC:ROWS_IN, :] = jnp.zeros((ROWS_IN - SPEC, C), f32)
    parts[ROWS_IN + C : LATE.first, :] = jnp.zeros((LATE.first - ROWS_IN - C, C), f32)
    parts[depth + 9 : PARTS, :] = jnp.zeros((PARTS - depth - 9, C), f32)

    keep_back.wait()
    all_back = cross(g_arrived.at[some], returned.at[some], BACK, place.sibling)
    all_back.wait_recv()

    def gathered(key):
        total = jnp.zeros((OBS, C), f32)
        for at in range(0, SLOTS, PART):
            index = lax.broadcasted_iota(i32, (PART, OBS), 0) + at
            pick = (index == key).astype(f32).astype(bf16)
            total = total + dot(pick, returned[at : at + PART, :], ((0,), (0,)))
        return total

    part[...] = gathered(slot_keys(route_sib[...], core, 1 - core)).astype(bf16)
    swap = cross(part, part_sib, SIB_PART, place.sibling)
    swap.start()
    own = gathered(slot_keys(route[...], core, core))
    parts[LATE.first : LATE.first + C, :] = dot(mixed[...], cot[...], ((0,), (0,)))
    swap.wait()
    g_emb[...] = (own + part_sib[...].astype(f32)).astype(bf16)
    parts[ROWS_IN : ROWS_IN + C, :] = dot(hidden[...], g_emb[...], ((0,), (0,)))
    g_hidden = dot(g_emb[...], w_out[...], ((1,), (1,)))
    pre = preact[...]
    sig = 1.0 / (1.0 + jnp.exp(-pre))
    g_pre = (g_hidden * sig * (1.0 + pre * (1.0 - sig))).astype(bf16)
    parts[0:SPEC, :] = dot(spec_t[...], g_pre, ((1,), (0,)))

    base = {EARLY: 0, LATE: EARLY.half}
    sems = {EARLY: ROUND_SEMS[0], LATE: ROUND_SEMS[1]}

    def half_of(r, which):
        return pl.ds(pl.multiple_of(r.first + which * r.half, 16), r.half)

    def local_half(r):
        return pl.ds(base[r], r.half)

    def swap_halves(r):
        swap_out[local_half(r), :] = parts[half_of(r, 1 - core), :].astype(bf16)
        copy = cross(swap_out.at[local_half(r)], swap_in.at[local_half(r)], sems[r][0], place.sibling)
        copy.start()
        return copy

    def owns(r, chip):
        return (chip >= r.owner) & (chip < r.owner + r.count)

    def send_blocks(r):
        rows_here = local_half(r)
        chip_sum[rows_here, :] = (
            parts[half_of(r, core), :] + swap_in[rows_here, :].astype(f32)
        ).astype(bf16)

        def own_block(chip):
            return chip_sum.at[pl.ds(pl.multiple_of(base[r] + (chip - r.owner) * 16, 16), 16)]

        def send(step, carry):
            chip, device = place.peer(step)

            @pl.when(owns(r, chip))
            def _():
                cross(own_block(chip), gather.at[me], sems[r][1], device).start()

            return carry

        lax.fori_loop(1, CHIPS, send, 0)

        @pl.when(owns(r, me))
        def _():
            pltpu.make_async_copy(own_block(me), gather.at[me], local_sem.at[3]).start()

    def share_sum(r):
        @pl.when(owns(r, me))
        def _():
            pltpu.make_async_copy(gather.at[me], gather.at[me], local_sem.at[3]).wait()
            cross(gather.at[few], gather.at[few], sems[r][1], place.sibling).wait_recv()
            owned[...] = jnp.sum(gather[...].astype(f32), axis=0).astype(bf16)
            here = pl.ds(
                pl.multiple_of(r.first + core * r.half + (me - r.owner) * 16, 16), 16
            )
            pltpu.make_async_copy(owned, result.at[here], local_sem.at[4]).start()

            def share(step, carry):
                _, device = place.peer(step)
                cross(owned, result.at[here], sems[r][2], device).start()
                return carry

            lax.fori_loop(1, CHIPS, share, 0)

    def collect(r):
        def waits(blocks):
            rows_here = pl.ds(0, blocks * 16)
            cross(chip_sum.at[rows_here], chip_sum.at[rows_here], sems[r][2], place.sibling).wait_recv()
            cross(chip_sum.at[rows_here], chip_sum.at[rows_here], sems[r][1], place.sibling).wait_send()

        @pl.when(owns(r, me))
        def _():
            pltpu.make_async_copy(owned, owned, local_sem.at[4]).wait()
            cross(gather.at[few], gather.at[few], sems[r][2], place.sibling).wait_send()
            waits(r.count - 1)

        @pl.when(jnp.logical_not(owns(r, me)))
        def _():
            waits(r.count)

        copy = cross(result.at[half_of(r, core)], result.at[half_of(r, core)], sems[r][3], place.sibling)
        copy.start()
        return copy

    early = swap_halves(EARLY)
    late = swap_halves(LATE)

    def point(i, carry):
        at = pl.ds(pl.multiple_of(i * 512, 512), 512)
        here = grid_ext[pl.ds(1 + 4 * i, 4)].astype(f32).reshape(512, C)
        latent[at, :] = (here + dot(mixed[at, :], w_point[...], ((1,), (0,)))).astype(bf16)
        return carry

    early.wait()
    send_blocks(EARLY)
    late.wait()
    send_blocks(LATE)
    lax.fori_loop(0, CLAT // 4, point, 0)
    share_sum(EARLY)
    share_sum(LATE)
    last = [collect(EARLY), collect(LATE)]
    for copy in (all_marks, all_data, all_back):
        copy.wait_send()
    for copy in last:
        copy.wait()


def run(spec_t, rows, w_in, w_out, w_point, w_depth, cot):
    dma = pltpu.SemaphoreType.DMA
    anywhere = pl.BlockSpec(memory_space=pl.ANY)
    field = VMEM((CLAT + 2, CLON, C), bf16)
    half = VMEM((EARLY.half + LATE.half, C), bf16)
    return pl.pallas_call(
        kernel,
        out_shape=[
            jax.ShapeDtypeStruct((CELLS, C), bf16),
            jax.ShapeDtypeStruct((PARTS, C), bf16),
        ],
        in_specs=[anywhere, vmem(), anywhere, anywhere, anywhere, vmem(), anywhere],
        out_specs=[vmem()] * 2,
        scratch_shapes=[
            VMEM((SPEC, OBS), bf16),
            VMEM((SPEC, C), bf16),
            VMEM((C, C), bf16),
            VMEM((C, C), bf16),
            VMEM((CELLS, C), bf16),
            VMEM((OBS, C), f32),
            VMEM((OBS, C), bf16),
            VMEM((OBS, C + META), bf16),
            VMEM((OBS, C + META), bf16),
            VMEM((8, OBS), i32),
            VMEM((8, OBS), i32),
            VMEM((SLOTS, C), bf16),
            VMEM((SLOTS, C), bf16),
            VMEM((CHIPS, 2, META), f32),
            VMEM((CHIPS, 2, META), f32),
            field,
            field,
            VMEM((4, CLAT, C), f32),
            VMEM((2, CLAT, C), bf16),
            VMEM((2, CLAT, C), bf16),
            VMEM((4, CLAT, C), bf16),
            VMEM((2, CLAT, C), bf16),
            VMEM((2, CLAT, C), bf16),
            VMEM((4, CLAT, C), bf16),
            VMEM((24, C), f32),
            VMEM((24, C), f32),
            VMEM((2, CLAT, 8, C), f32),
            VMEM((CELLS, C), bf16),
            VMEM((SLOTS, C), bf16),
            VMEM((SLOTS, C), bf16),
            VMEM((OBS, C), bf16),
            VMEM((OBS, C), bf16),
            VMEM((OBS, C), bf16),
            VMEM((CELLS, C), bf16),
            VMEM((PARTS, C), f32),
            half,
            half,
            half,
            VMEM((CHIPS, 16, C), bf16),
            VMEM((16, C), bf16),
            dma((5,)),
            dma((5,)),
            dma((SEMS,)),
            dma((SEMS,)),
            dma((2, 8)),
            dma((2, 8)),
        ],
        compiler_params=pltpu.CompilerParams(
            collective_id=0, has_side_effects=True, vmem_limit_bytes=60 << 20
        ),
    )(spec_t, rows, w_in, w_out, w_point, w_depth, cot)


def on_device(spectra, owner, cell, w_in, w_out, w_point, w_depth, cotangent):
    zero = jnp.zeros((13, OBS), bf16)
    rows = jnp.concatenate(
        [jnp.stack([owner[:, 0], cell // 16, cell % 16]).astype(bf16), zero], axis=0
    )
    latent, total = run(
        spectra.T, rows, w_in, w_out, w_point, w_depth, cotangent.reshape(CELLS, C)
    )
    total = total.astype(f32)
    tiles = N_LAT * N_LON
    obs_scale = 1.0 / jnp.sqrt(f32(OBS * tiles))
    cell_scale = 1.0 / jnp.sqrt(f32(CELLS * tiles))
    at = ROWS_IN
    late = LATE.first
    return (
        latent.reshape(CLAT, CLON, C),
        total[:SPEC] * obs_scale,
        total[at : at + C] * obs_scale,
        total[late : late + C] * cell_scale,
        total[late + C : late + C + 9] * cell_scale,
    )


def solution(mesh):
    in_specs = (
        P(("lat", "lon"), None),
        P(("lat", "lon"), None),
        P(("lat", "lon")),
        P(),
        P(),
        P(),
        P(),
        P("lat", "lon", None),
    )
    out_specs = (P("lat", "lon", None), P(), P(), P(), P())
    return jax.shard_map(
        on_device, mesh=mesh, in_specs=in_specs, out_specs=out_specs, check_vma=False
    )
```

time: 321 us -> 106 us (0.33)
  waiting for transfers between devices: 113 us -> 0 us
  Pallas kernels: 0 us -> 95.9 us
  blocking collectives: 67.8 us -> 0 us
  starting transfers between devices: 49 us -> 0 us
  matrix products: 33 us -> 0 us
  other arithmetic: 33.3 us -> 7.28 us
  between operations: 14.4 us -> 0.66 us
  local copies, waits for them, and re-layouts: 10.5 us -> 1.51 us
    pallas_call x0 -> x1, Pallas kernels: none -> 95.9 us  [run(): pl.pallas_call(kernel, out_shape=[jax.ShapeDtypeStruct((CELLS, C), bf16),...]
    psum x1 -> x0, waiting for transfers between devices: 82.1 us -> none  [on_device(): lax.psum((grad_in, grad_out, grad_point, grad_depth), ('lat', 'lon'))]
    psum x1 -> x0, blocking collectives: 67.8 us -> none  [on_device(): lax.psum((grad_in, grad_out, grad_point, grad_depth), ('lat', 'lon'))]
    dot_general x9 -> x0, matrix products: 33 us -> none  [the longest x1 8.6 us: on_device(): jnp.dot(cot_rows, w_point.T, preferred_element_type=jnp.float32)]
    all_to_all x3 -> x0, starting transfers between devices: 27.2 us -> none  [the longest x1 11.5 us: send_out(): lax.all_to_all(places.reshape(tiles, cap), ('lat', 'lon'), split_axis=0,...]
    convert_element_type x4 -> x1, other arithmetic: 24.3 us -> 1.94 us  [on_device(): total = total.astype(f32)]
    ppermute x8 -> x0, starting transfers between devices: 21.5 us -> none  [the longest x4 13.3 us: extended(): lax.ppermute(lax.slice_in_dim(block, 0, width, axis=dim), axis, backward)]
    all_to_all x3 -> x0, waiting for transfers between devices: 19.3 us -> none  [the longest x1 17.4 us: send_out(): lax.all_to_all(values.reshape(tiles, cap, width), ('lat', 'lon'), split_a...]
  transfers between devices with their start and end apart: 12 -> 0, of which waited for: 7 -> 0; matrix products, arithmetic and copies ran while one was open for 11% -> 0% of each run, Pallas kernels for 0% -> 0%
where the time goes in v2:
time: 106 us; the launch traced here: 105 us
  Pallas kernels  95.9 us (90%)
  other arithmetic  7.28 us (7%)
  local copies, waits for them, and re-layouts  1.51 us (1%)
    pallas_call x1, Pallas kernels, run(): pl.pallas_call(kernel, out_shape=[jax.ShapeDtypeStruct((CELLS, C), bf16),...  95.9 us

profile of v2, /device:TPU:1, one launch (start us, length us, event | category | flops | bytes accessed | tf_op | source)
XLA Modules:
  0.0 105.3 jit_solution(16946076377719587919)
XLA Ops:
  0.6 0.7 fusion.5
  1.3 0.7 convert_bitcast_fusion
  2.0 0.6 fusion.4.rows
  2.6 95.9 %shard_map.119 = (bf16[2048,512]{1,0:T(8,128)(2,1)}, bf16[1696,512]{1,0:T(8,128)(2,1)}) custom-call(bf16[616,512]{1,0:T(8,128)(2,1)} %bitcast.7, bf16[16,512]{1,0:T(8,128)(2,1)} %fusion.4.rows, bf16[616,512]{1,0:T(8,128)(2,1)} %w_in_in.1, bf16[512,512]{1,0:T(8,128)(2,1)} %w_out_in.1, bf16[512,512]{1,0:T(8,128)(2,1)} %w_point_in.1, f32[9,512]{1,0:T(8,128)} %w_depth.1, ...), custom_call_target="tpu_custom_call" | custom-call | tf_op jit(solution)/shard_map/pallas_call | solution.py:644
  98.5 1.9 %convert_element_type.4 = f32[1696,512]{1,0:T(8,128)S(1)} convert(bf16[1696,512]{1,0:T(8,128)(2,1)} %get-tuple-element.8) | non-fusion elementwise | flops 868352 | bytes 5210112 | tf_op jit(solution)/shard_map/convert_element_type | solution.py:714
  100.5 1.2 %slice_multiply_fusion = f32[616,512]{1,0:T(8,128)} fusion(f32[1696,512]{1,0:T(8,128)S(1)} %convert_element_type.4), kind=kLoop, calls=%fused_computation | loop fusion | flops 315392 | bytes 2523136 | tf_op jit(solution)/shard_map/mul | solution.py:722
  101.6 0.0 copy-start
  101.7 1.5 %slice_multiply_fusion.1 = (f32[512,512]{1,0:T(8,128)}, f32[512,512]{1,0:T(8,128)}) fusion(f32[1696,512]{1,0:T(8,128)S(1)} %convert_element_type.4), kind=kLoop, calls=%fused_computation.1 | loop fusion | flops 524288 | bytes 4194304 | tf_op jit(solution)/shard_map/mul | solution.py:724
  103.2 0.6 slice_multiply_fusion.3
  103.8 0.2 copy-done
  104.0 1.3 %copy.14 = bf16[16,128,512]{2,1,0:T(8,128)(2,1)} copy(bf16[16,128,512]{2,1,0:T(8,128)(2,1)S(1)} %bitcast.6) | data formatting | bytes 4194304
  (2 shorter events, 0.0 us)
Async XLA Ops:
  101.6 2.3 %copy-start = (bf16[2048,512]{1,0:T(8,128)(2,1)S(1)}, bf16[2048,512]{1,0:T(8,128)(2,1)}, u32[]{:S(2)}) copy-start(bf16[2048,512]{1,0:T(8,128)(2,1)} %get-tuple-element.7) | copy-start | bytes 6291460

commit v3 on v2

--- a/solution.py
+++ b/solution.py
@@ -1,4 +1,4 @@
-import functools
+import math
 
 import jax
 import jax.numpy as jnp
@@ -21,7 +21,7 @@
 CELLS = CLAT * CLON
 SPEC = 616
 META = 128
-ROWS_IN = 624
+ROWS_IN = 640
 PART = 256
 CHUNK = 128
 
@@ -68,7 +68,7 @@
     )
 
 
-def greet(place, halo):
+def greet(place):
     barrier = pltpu.get_barrier_semaphore()
 
     def hello(device):
@@ -81,19 +81,19 @@
         return carry
 
     lax.fori_loop(1, CHIPS, one, 0)
-    if not halo:
-        hello(place.sibling)
-        return barrier, CHIPS
+    others = N_LAT // 2
+    for x in range(others):
+        hello((2 * x + 1 - place.core, place.lon))
     for side in (-1, 1):
         inside = (place.lat + side >= 0) & (place.lat + side < N_LAT)
 
         @pl.when(inside)
         def _(side=side):
-            for turn in (-1, 0, 1):
+            for turn in (-1, 1):
                 hello((place.lat + side, (place.lon + turn + N_LON) % N_LON))
 
     edges = (place.lat > 0).astype(i32) + (place.lat < N_LAT - 1).astype(i32)
-    return barrier, CHIPS - 1 + 3 * edges
+    return barrier, CHIPS - 1 + others + 2 * edges
 
 
 class Halo:
@@ -149,13 +149,16 @@
             self.to_diag[3] = jnp.zeros((CLAT, C), bf16)
 
 
-def vector_encode(spec_t, rows, w_in, w_out, preact, hidden, emb, route):
+def vector_encode(spec_t, owner, cell, w_in, w_out, preact, hidden, emb, route, table):
     pre = dot(spec_t[...], w_in[...], ((0,), (0,)))
     preact[...] = pre
     hid = (pre * (1.0 / (1.0 + jnp.exp(-pre)))).astype(bf16)
     hidden[...] = hid
     emb[:, :C] = dot(hid, w_out[...], ((1,), (0,))).astype(bf16)
-    values = rows[...]
+    places = cell[...]
+    values = jnp.concatenate(
+        [owner[...], places // 16, places % 16, jnp.zeros((13, OBS), i32)], axis=0
+    ).astype(f32).astype(bf16)
     down = lax.broadcasted_iota(i32, (OBS, OBS), 0)
     across = lax.broadcasted_iota(i32, (OBS, OBS), 1)
     eye = (down == across).astype(f32).astype(bf16)
@@ -176,6 +179,7 @@
     value = jnp.where(kind == 0, high_col, jnp.where(kind == 1, low_col, 1.0))
     keep = (lane % CAP == pos_col) & (kind < 3)
     emb[:, C:] = jnp.where(keep, value, 0.0).astype(bf16)
+    table[...] = dot(hits_t.astype(bf16), emb[:, C:], ((1,), (0,))).reshape(N_LAT, N_LON, META)
     tile = tile_row.astype(i32)
     lat, lon = tile // N_LON, tile % N_LON
     chip = lat // 2 * N_LON + lon
@@ -189,18 +193,39 @@
 
 
 class Round:
-    def __init__(self, first, count, owner):
-        self.first, self.count, self.owner = first, count, owner
-        self.half = count * 16
-
-
-EARLY = Round(0, 36, 0)
-LATE = Round(1152, 17, 36)
-PARTS = 1152 + 544
-
-SIB_EMB, SIB_ROUTE, MARK, DATA, BACK, SIB_PART = range(6)
-ROUND_SEMS = ((6, 7, 8, 9), (10, 11, 12, 13))
-SEMS = 14
+    def __init__(self, number, axis, first, quarter, width):
+        self.axis, self.first, self.quarter, self.width = axis, first, quarter, width
+        self.half = 4 * quarter
+        self.base = first // 2
+        self.across = C // width
+        self.count = quarter // 16 * self.across
+        self.sems = range(7 + 6 * number, 13 + 6 * number)
+
+    def line(self, place):
+        x, z, y, core = place.x, place.lon // SIDE, place.lon % SIDE, place.core
+        if self.axis == "x":
+            return x, lambda q: (2 * q + core, place.lon)
+        if self.axis == "y":
+            return y, lambda q: (place.lat, z * SIDE + q)
+        return z, lambda q: (place.lat, q * SIDE + y)
+
+    def plane(self, place):
+        x, z, y, core = place.x, place.lon // SIDE, place.lon % SIDE, place.core
+        if self.axis == "x":
+            return place.lon, lambda m: (place.lat, m)
+        if self.axis == "y":
+            return x * SIDE + z, lambda m: (2 * (m // SIDE) + core, m % SIDE * SIDE + y)
+        return x * SIDE + y, lambda m: (2 * (m // SIDE) + core, z * SIDE + m % SIDE)
+
+
+IN = Round(0, "z", 0, 80, 256)
+OUT = Round(1, "y", 640, 64, 128)
+POINT = Round(2, "x", 1152, 64, 128)
+PARTS = 1664
+DEPTH = 624
+
+SIB_EMB, SIB_ROUTE, MARK_LAT, MARK_LON, DATA, BACK, SIB_PART = range(7)
+SEMS = 7 + 18
 
 
 def block(ref, chip, size=SLOT):
@@ -246,7 +271,8 @@
 
 def kernel(
     spec_in,
-    rows,
+    owner,
+    cell,
     w_in_in,
     w_out_in,
     w_point_in,
@@ -267,6 +293,8 @@
     route_sib,
     outgoing,
     arrived,
+    table,
+    table_lat,
     marks,
     places,
     gm_ext,
@@ -292,8 +320,16 @@
     swap_out,
     swap_in,
     chip_sum,
-    gather,
-    owned,
+    lines_in,
+    lines_out,
+    lines_point,
+    quarter_in,
+    quarter_out,
+    quarter_point,
+    gather_in,
+    gather_out,
+    gather_point,
+    latent_here,
     load_sem,
     local_sem,
     send_sem,
@@ -317,7 +353,7 @@
     ]
     for copy in loads:
         copy.start()
-    barrier, count = greet(place, True)
+    barrier, count = greet(place)
 
     def cross(src, dst, index, device):
         return remote(src, dst, send_sem.at[index], recv_sem.at[index], device)
@@ -328,7 +364,7 @@
     halo_x.clear_outside()
     for copy in loads[:3]:
         copy.wait()
-    vector_encode(spec_t, rows, w_in, w_out, preact, hidden, emb, route)
+    vector_encode(spec_t, owner, cell, w_in, w_out, preact, hidden, emb, route, table)
     for copy in loads[3:]:
         copy.wait()
 
@@ -349,6 +385,13 @@
     ]
     for copy in swaps:
         copy.start()
+    keep_lat = pltpu.make_async_copy(
+        table.at[place.lat], table_lat.at[place.lat], local_sem.at[5]
+    )
+    keep_lat.start()
+    for step in range(1, N_LAT):
+        lat = (place.lat + step) % N_LAT
+        cross(table.at[lat], table_lat.at[place.lat], MARK_LAT, (lat, place.lon)).start()
     halo_g.start()
 
     def spread(key, values, more):
@@ -364,33 +407,23 @@
 
         lax.fori_loop(0, SLOTS // PART, one, 0)
 
-    chips = lax.broadcasted_iota(i32, (CHIPS, OBS), 0)
-
-    def marked(info, values):
-        wanted = (info[2:3, :] == chips) & (info[1:2, :] == core)
-        return dot(wanted.astype(f32).astype(bf16), values[:, C:], ((1,), (0,)))
-
     spread(slot_keys(route[...], core, core), emb, False)
-    own = marked(route, emb)
+    keep_lat.wait()
+    lat_row = pl.ds(0, N_LAT - 1)
+    lat_marks = cross(table.at[lat_row], table_lat.at[lat_row], MARK_LAT, place.sibling)
+    lat_marks.wait_recv()
+    for lon in range(N_LON):
+        marks[lon] = table_lat[:, lon, :]
+    keep_lon = pltpu.make_async_copy(marks.at[place.lon], places.at[place.lon], local_sem.at[0])
+    keep_lon.start()
+    for step in range(1, N_LON):
+        lon = (place.lon + step) % N_LON
+        cross(marks.at[lon], places.at[place.lon], MARK_LON, (place.lat, lon)).start()
     for copy in swaps:
         copy.wait()
-    other = marked(route_sib, emb_sib)
-    marks[:, 0, :] = jnp.where(core == 0, own, other)
-    marks[:, 1, :] = jnp.where(core == 0, other, own)
     spread(slot_keys(route_sib[...], core, 1 - core), emb_sib, True)
-    keep = [
-        pltpu.make_async_copy(marks.at[me], places.at[me], local_sem.at[0]),
-        pltpu.make_async_copy(block(outgoing, me), block(arrived, me), local_sem.at[1]),
-    ]
-    for copy in keep:
-        copy.start()
-
-    def send_marks(step, carry):
-        chip, device = place.peer(step)
-        cross(marks.at[chip], places.at[me], MARK, device).start()
-        return carry
-
-    lax.fori_loop(1, CHIPS, send_marks, 0)
+    keep = pltpu.make_async_copy(block(outgoing, me), block(arrived, me), local_sem.at[1])
+    keep.start()
 
     def send_data(step, carry):
         chip, device = place.peer(step)
@@ -416,32 +449,31 @@
 
     lax.fori_loop(0, CLAT, conv_back, 0)
 
-    for copy in keep:
-        copy.wait()
-    all_marks = cross(marks.at[few], places.at[few], MARK, place.sibling)
-    all_marks.wait_recv()
-    tables = [places[:, k, :].astype(bf16) for k in range(2)]
-    down = lax.broadcasted_iota(i32, (SLOTS, CHIPS), 0)
-    expand = (down // SLOT == lax.broadcasted_iota(i32, (SLOTS, CHIPS), 1)).astype(f32).astype(bf16)
-    slot = lax.broadcasted_iota(i32, (SLOTS, META), 0)
-    lane = lax.broadcasted_iota(i32, (SLOTS, META), 1)
-    wide = [dot(expand, table, ((1,), (0,))) for table in tables]
-    mine = jnp.where((slot // CAP) % 2 == 0, wide[0], wide[1])
-    factor = jnp.where(lane < CAP, 16.0, 1.0)
-    place_col = (
-        jnp.sum(jnp.where(lane % CAP == slot % CAP, mine * factor, 0.0), axis=1, keepdims=True) - 1.0
-    ).astype(i32)
-    across = lax.broadcasted_iota(i32, (CHIPS, SLOTS), 1)
-    expand_t = (across // SLOT == lax.broadcasted_iota(i32, (CHIPS, SLOTS), 0)).astype(f32).astype(bf16)
-    slot_t = lax.broadcasted_iota(i32, (META, SLOTS), 1)
-    lane_t = lax.broadcasted_iota(i32, (META, SLOTS), 0)
-    wide_t = [dot(table, expand_t, ((0,), (0,))) for table in tables]
-    mine_t = jnp.where((slot_t // CAP) % 2 == 0, wide_t[0], wide_t[1])
-    factor_t = jnp.where(lane_t < CAP, 16.0, 1.0)
-    place_row = (
-        jnp.sum(jnp.where(lane_t % CAP == slot_t % CAP, mine_t * factor_t, 0.0), axis=0, keepdims=True)
-        - 1.0
-    ).astype(i32)
+    keep_lon.wait()
+    lon_row = pl.ds(0, N_LON - 1)
+    lon_marks = cross(marks.at[lon_row], places.at[lon_row], MARK_LON, place.sibling)
+    lon_marks.wait_recv()
+    tiles = N_LAT * N_LON
+    known = places[...].reshape(tiles, META).astype(bf16)
+
+    def sender(slot):
+        chip = slot // SLOT
+        return chip % N_LON * N_LAT + chip // N_LON * 2 + slot // CAP % 2
+
+    def cells_of(axis):
+        shape = (SLOTS, tiles) if axis == 0 else (tiles, SLOTS)
+        slot = lax.broadcasted_iota(i32, shape, axis)
+        other = lax.broadcasted_iota(i32, shape, 1 - axis)
+        expand = (sender(slot) == other).astype(f32).astype(bf16)
+        if axis == 0:
+            wide = dot(expand, known, ((1,), (0,)))
+        else:
+            wide = dot(known, expand, ((0,), (0,)))
+        value = jnp.where(other < CAP, 16.0, 1.0) * wide
+        keep = jnp.where(other % CAP == slot % CAP, value, 0.0)
+        return (jnp.sum(keep, axis=1 - axis, keepdims=True) - 1.0).astype(i32)
+
+    place_col, place_row = cells_of(0), cells_of(1)
     cells = lax.broadcasted_iota(i32, (PART, CELLS), 1)
     for at in range(0, SLOTS, PART):
         pick = (place_col[at : at + PART] == cells).astype(f32).astype(bf16)
@@ -458,6 +490,7 @@
 
     all_data = cross(outgoing.at[some], arrived.at[some], DATA, place.sibling)
     all_data.wait_recv()
+    keep.wait()
 
     def bin_rows(i, carry):
         index = lax.broadcasted_iota(i32, (PART, SLOTS), 0) + i * PART
@@ -473,7 +506,6 @@
     halo_x.wait()
     side_columns(to_cols_x, to_diag_x, west, east)
     side_sums(west, east, lambda k: w_depth[k : k + 1, :], sides)
-    depth = LATE.first + C
     for chunk in range(C // CHUNK):
         lanes = slice(chunk * CHUNK, (chunk + 1) * CHUNK)
 
@@ -502,10 +534,136 @@
                 side = (west if b < 0 else east)[1 + a : 1 + a + CLAT, lanes]
                 edge = cols_f[0 if b < 0 else 1, :, lanes].astype(bf16).astype(f32)
                 total = total + jnp.sum(side * edge, axis=0, keepdims=True)
-            parts[depth + k : depth + k + 1, lanes] = total
-    parts[SPEC:ROWS_IN, :] = jnp.zeros((ROWS_IN - SPEC, C), f32)
-    parts[ROWS_IN + C : LATE.first, :] = jnp.zeros((LATE.first - ROWS_IN - C, C), f32)
-    parts[depth + 9 : PARTS, :] = jnp.zeros((PARTS - depth - 9, C), f32)
+            parts[DEPTH + k : DEPTH + k + 1, lanes] = total
+    parts[SPEC:DEPTH, :] = jnp.zeros((DEPTH - SPEC, C), f32)
+    parts[DEPTH + 9 : ROWS_IN, :] = jnp.zeros((ROWS_IN - DEPTH - 9, C), f32)
+    parts[POINT.first : PARTS, :] = dot(mixed[...], cot[...], ((0,), (0,)))
+
+    lines = {IN: lines_in, OUT: lines_out, POINT: lines_point}
+    quarter = {IN: quarter_in, OUT: quarter_out, POINT: quarter_point}
+    gathers = {IN: gather_in, OUT: gather_out, POINT: gather_point}
+
+    def half_of(r, which):
+        return pl.ds(pl.multiple_of(r.first + which * r.half, 16), r.half)
+
+    def local_half(r):
+        return pl.ds(r.base, r.half)
+
+    def swap_halves(r):
+        swap_out[local_half(r), :] = parts[half_of(r, 1 - core), :].astype(bf16)
+        copy = cross(swap_out.at[local_half(r)], swap_in.at[local_half(r)], r.sems[0], place.sibling)
+        copy.start()
+        return copy
+
+    def rows_at(start, size):
+        return pl.ds(pl.multiple_of(start, 16), size)
+
+    def send_line(r):
+        here = local_half(r)
+        chip_sum[here, :] = (
+            parts[half_of(r, core), :] + swap_in[here, :].astype(f32)
+        ).astype(bf16)
+        at, device = r.line(place)
+        for step in range(1, 4):
+            q = (at + step) % 4
+            src = chip_sum.at[rows_at(r.base + q * r.quarter, r.quarter)]
+            cross(src, lines[r].at[at], r.sems[1], device(q)).start()
+
+    def piece(r, start, index):
+        rows_here = rows_at(start + index // r.across * 16, 16)
+        return rows_here, pl.ds(pl.multiple_of(index % r.across * r.width, 128), r.width)
+
+    def waiting(r, size, sem):
+        some = gathers[r].at[pl.ds(0, size)]
+        return cross(some, some, r.sems[sem], place.sibling)
+
+    def waiting_line(r, sem):
+        some = lines[r].at[pl.ds(0, 3)]
+        return cross(some, some, r.sems[sem], place.sibling)
+
+    def send_plane(r):
+        waiting_line(r, 1).wait_recv()
+        at, _ = r.line(place)
+        total = chip_sum[rows_at(r.base + at * r.quarter, r.quarter), :].astype(f32)
+        for step in range(1, 4):
+            total = total + lines[r][(at + step) % 4].astype(f32)
+        quarter[r][...] = total.astype(bf16)
+        me_here, device = r.plane(place)
+
+        def send(step, carry):
+            index = (me_here + step) % 16
+
+            @pl.when(index < r.count)
+            def _():
+                where = piece(r, 0, index)
+                cross(quarter[r].at[where], gathers[r].at[me_here], r.sems[2], device(index)).start()
+
+            return carry
+
+        lax.fori_loop(1, 16, send, 0)
+
+    def result_rows(r):
+        return r.first + core * r.half + r.line(place)[0] * r.quarter
+
+    def share_plane(r):
+        me_here, device = r.plane(place)
+
+        @pl.when(me_here < r.count)
+        def _():
+            waiting(r, 15, 2).wait_recv()
+            total = quarter[r][piece(r, 0, me_here)].astype(f32)
+            for step in range(1, 16):
+                total = total + gathers[r][(me_here + step) % 16].astype(f32)
+            where = piece(r, result_rows(r), me_here)
+            result[where] = total.astype(bf16)
+
+            def share(step, carry):
+                index = (me_here + step) % 16
+                cross(result.at[where], result.at[where], r.sems[3], device(index)).start()
+                return carry
+
+            lax.fori_loop(1, 16, share, 0)
+
+    def share_line(r):
+        me_here, _ = r.plane(place)
+        if r.count == 16:
+            waiting(r, 15, 3).wait_recv()
+        else:
+            pl.when(me_here < r.count)(lambda: waiting(r, r.count - 1, 3).wait_recv())
+            pl.when(me_here >= r.count)(lambda: waiting(r, r.count, 3).wait_recv())
+        at, device = r.line(place)
+        here = result.at[rows_at(result_rows(r), r.quarter)]
+        for step in range(1, 4):
+            cross(here, here, r.sems[4], device((at + step) % 4)).start()
+
+    def last_swap(r):
+        waiting_line(r, 4).wait_recv()
+        half = result.at[half_of(r, core)]
+        copy = cross(half, half, r.sems[5], place.sibling)
+        copy.start()
+        return copy
+
+    def sent(r):
+        waiting_line(r, 1).wait_send()
+        waiting_line(r, 4).wait_send()
+        me_here, _ = r.plane(place)
+
+        def owner():
+            waiting(r, r.count - 1, 2).wait_send()
+            waiting(r, 15, 3).wait_send()
+
+        if r.count == 16:
+            owner()
+        else:
+            pl.when(me_here < r.count)(owner)
+            pl.when(me_here >= r.count)(lambda: waiting(r, r.count, 2).wait_send())
+
+    def point(i):
+        at = slice(i * 512, (i + 1) * 512)
+        here = grid_ext[1 + 4 * i : 5 + 4 * i].astype(f32).reshape(512, C)
+        latent_here[at, :] = (here + dot(mixed[at, :], w_point[...], ((1,), (0,)))).astype(bf16)
+
+    point_swap = swap_halves(POINT)
 
     keep_back.wait()
     all_back = cross(g_arrived.at[some], returned.at[some], BACK, place.sibling)
@@ -523,132 +681,60 @@
     swap = cross(part, part_sib, SIB_PART, place.sibling)
     swap.start()
     own = gathered(slot_keys(route[...], core, core))
-    parts[LATE.first : LATE.first + C, :] = dot(mixed[...], cot[...], ((0,), (0,)))
     swap.wait()
     g_emb[...] = (own + part_sib[...].astype(f32)).astype(bf16)
-    parts[ROWS_IN : ROWS_IN + C, :] = dot(hidden[...], g_emb[...], ((0,), (0,)))
+    parts[OUT.first : OUT.first + C, :] = dot(hidden[...], g_emb[...], ((0,), (0,)))
+    out_swap = swap_halves(OUT)
     g_hidden = dot(g_emb[...], w_out[...], ((1,), (1,)))
     pre = preact[...]
     sig = 1.0 / (1.0 + jnp.exp(-pre))
     g_pre = (g_hidden * sig * (1.0 + pre * (1.0 - sig))).astype(bf16)
     parts[0:SPEC, :] = dot(spec_t[...], g_pre, ((1,), (0,)))
-
-    base = {EARLY: 0, LATE: EARLY.half}
-    sems = {EARLY: ROUND_SEMS[0], LATE: ROUND_SEMS[1]}
-
-    def half_of(r, which):
-        return pl.ds(pl.multiple_of(r.first + which * r.half, 16), r.half)
-
-    def local_half(r):
-        return pl.ds(base[r], r.half)
-
-    def swap_halves(r):
-        swap_out[local_half(r), :] = parts[half_of(r, 1 - core), :].astype(bf16)
-        copy = cross(swap_out.at[local_half(r)], swap_in.at[local_half(r)], sems[r][0], place.sibling)
-        copy.start()
-        return copy
-
-    def owns(r, chip):
-        return (chip >= r.owner) & (chip < r.owner + r.count)
-
-    def send_blocks(r):
-        rows_here = local_half(r)
-        chip_sum[rows_here, :] = (
-            parts[half_of(r, core), :] + swap_in[rows_here, :].astype(f32)
-        ).astype(bf16)
-
-        def own_block(chip):
-            return chip_sum.at[pl.ds(pl.multiple_of(base[r] + (chip - r.owner) * 16, 16), 16)]
-
-        def send(step, carry):
-            chip, device = place.peer(step)
-
-            @pl.when(owns(r, chip))
-            def _():
-                cross(own_block(chip), gather.at[me], sems[r][1], device).start()
-
-            return carry
-
-        lax.fori_loop(1, CHIPS, send, 0)
-
-        @pl.when(owns(r, me))
-        def _():
-            pltpu.make_async_copy(own_block(me), gather.at[me], local_sem.at[3]).start()
-
-    def share_sum(r):
-        @pl.when(owns(r, me))
-        def _():
-            pltpu.make_async_copy(gather.at[me], gather.at[me], local_sem.at[3]).wait()
-            cross(gather.at[few], gather.at[few], sems[r][1], place.sibling).wait_recv()
-            owned[...] = jnp.sum(gather[...].astype(f32), axis=0).astype(bf16)
-            here = pl.ds(
-                pl.multiple_of(r.first + core * r.half + (me - r.owner) * 16, 16), 16
-            )
-            pltpu.make_async_copy(owned, result.at[here], local_sem.at[4]).start()
-
-            def share(step, carry):
-                _, device = place.peer(step)
-                cross(owned, result.at[here], sems[r][2], device).start()
-                return carry
-
-            lax.fori_loop(1, CHIPS, share, 0)
-
-    def collect(r):
-        def waits(blocks):
-            rows_here = pl.ds(0, blocks * 16)
-            cross(chip_sum.at[rows_here], chip_sum.at[rows_here], sems[r][2], place.sibling).wait_recv()
-            cross(chip_sum.at[rows_here], chip_sum.at[rows_here], sems[r][1], place.sibling).wait_send()
-
-        @pl.when(owns(r, me))
-        def _():
-            pltpu.make_async_copy(owned, owned, local_sem.at[4]).wait()
-            cross(gather.at[few], gather.at[few], sems[r][2], place.sibling).wait_send()
-            waits(r.count - 1)
-
-        @pl.when(jnp.logical_not(owns(r, me)))
-        def _():
-            waits(r.count)
-
-        copy = cross(result.at[half_of(r, core)], result.at[half_of(r, core)], sems[r][3], place.sibling)
-        copy.start()
-        return copy
-
-    early = swap_halves(EARLY)
-    late = swap_halves(LATE)
-
-    def point(i, carry):
-        at = pl.ds(pl.multiple_of(i * 512, 512), 512)
-        here = grid_ext[pl.ds(1 + 4 * i, 4)].astype(f32).reshape(512, C)
-        latent[at, :] = (here + dot(mixed[at, :], w_point[...], ((1,), (0,)))).astype(bf16)
-        return carry
-
-    early.wait()
-    send_blocks(EARLY)
-    late.wait()
-    send_blocks(LATE)
-    lax.fori_loop(0, CLAT // 4, point, 0)
-    share_sum(EARLY)
-    share_sum(LATE)
-    last = [collect(EARLY), collect(LATE)]
-    for copy in (all_marks, all_data, all_back):
+    in_swap = swap_halves(IN)
+    point_swap.wait()
+    send_line(POINT)
+    out_swap.wait()
+    send_line(OUT)
+    in_swap.wait()
+    send_line(IN)
+    point(0)
+    send_plane(POINT)
+    send_plane(OUT)
+    send_plane(IN)
+    point(1)
+    share_plane(POINT)
+    share_plane(OUT)
+    share_plane(IN)
+    point(2)
+    share_line(POINT)
+    share_line(OUT)
+    share_line(IN)
+    point(3)
+    store = pltpu.make_async_copy(latent_here, latent, local_sem.at[6])
+    store.start()
+    last = [last_swap(POINT), last_swap(OUT), last_swap(IN)]
+    for r in (POINT, OUT, IN):
+        sent(r)
+    store.wait()
+    for copy in (lat_marks, lon_marks, all_data, all_back):
         copy.wait_send()
     for copy in last:
         copy.wait()
 
 
-def run(spec_t, rows, w_in, w_out, w_point, w_depth, cot):
+def run(spec_t, owner, cell, w_in, w_out, w_point, w_depth, cot):
     dma = pltpu.SemaphoreType.DMA
     anywhere = pl.BlockSpec(memory_space=pl.ANY)
     field = VMEM((CLAT + 2, CLON, C), bf16)
-    half = VMEM((EARLY.half + LATE.half, C), bf16)
+    half = VMEM((PARTS // 2, C), bf16)
     return pl.pallas_call(
         kernel,
         out_shape=[
             jax.ShapeDtypeStruct((CELLS, C), bf16),
             jax.ShapeDtypeStruct((PARTS, C), bf16),
         ],
-        in_specs=[anywhere, vmem(), anywhere, anywhere, anywhere, vmem(), anywhere],
-        out_specs=[vmem()] * 2,
+        in_specs=[anywhere, vmem(), vmem(), anywhere, anywhere, anywhere, vmem(), anywhere],
+        out_specs=[anywhere, vmem()],
         scratch_shapes=[
             VMEM((SPEC, OBS), bf16),
             VMEM((SPEC, C), bf16),
@@ -663,8 +749,10 @@
             VMEM((8, OBS), i32),
             VMEM((SLOTS, C), bf16),
             VMEM((SLOTS, C), bf16),
-            VMEM((CHIPS, 2, META), f32),
-            VMEM((CHIPS, 2, META), f32),
+            VMEM((N_LAT, N_LON, META), f32),
+            VMEM((N_LAT, N_LON, META), f32),
+            VMEM((N_LON, N_LAT, META), f32),
+            VMEM((N_LON, N_LAT, META), f32),
             field,
             field,
             VMEM((4, CLAT, C), f32),
@@ -688,10 +776,14 @@
             half,
             half,
             half,
-            VMEM((CHIPS, 16, C), bf16),
-            VMEM((16, C), bf16),
+        ]
+        + [VMEM((4, r.quarter, C), bf16) for r in (IN, OUT, POINT)]
+        + [VMEM((r.quarter, C), bf16) for r in (IN, OUT, POINT)]
+        + [VMEM((16, 16, r.width), bf16) for r in (IN, OUT, POINT)]
+        + [
+            VMEM((CELLS, C), bf16),
             dma((5,)),
-            dma((5,)),
+            dma((7,)),
             dma((SEMS,)),
             dma((SEMS,)),
             dma((2, 8)),
@@ -700,30 +792,70 @@
         compiler_params=pltpu.CompilerParams(
             collective_id=0, has_side_effects=True, vmem_limit_bytes=60 << 20
         ),
-    )(spec_t, rows, w_in, w_out, w_point, w_depth, cot)
+    )(spec_t, owner, cell, w_in, w_out, w_point, w_depth, cot)
+
+
+def finish_kernel(
+    latent_in, total_in, latent, g_in, g_out, g_point, g_depth, total, in_f, out_f, point_f, latent_here, sem
+):
+    obs_scale = 1.0 / math.sqrt(OBS * N_LAT * N_LON)
+    cell_scale = 1.0 / math.sqrt(CELLS * N_LAT * N_LON)
+    plan = (
+        (in_f, g_in, IN.first, 640, obs_scale),
+        (out_f, g_out, OUT.first, C, obs_scale),
+        (point_f, g_point, POINT.first, C, cell_scale),
+    )
+    loads = []
+    for i, (_, _, first, size, _) in enumerate(plan):
+        rows = pl.ds(first, size)
+        loads.append(pltpu.make_async_copy(total_in.at[rows], total.at[rows], sem.at[i]))
+    loads.append(pltpu.make_async_copy(latent_in, latent_here, sem.at[3]))
+    for copy in loads:
+        copy.start()
+    copies = []
+    for i, (values, target, first, _, scale) in enumerate(plan):
+        loads[i].wait()
+        values[...] = total[first : first + values.shape[0], :].astype(f32) * scale
+        copies.append(pltpu.make_async_copy(values, target, sem.at[4 + i]))
+        copies[-1].start()
+        if i == 0:
+            g_depth[...] = total[DEPTH : DEPTH + 16, :].astype(f32)[0:9] * cell_scale
+    loads[3].wait()
+    copies.append(pltpu.make_async_copy(latent_here, latent, sem.at[7]))
+    copies[-1].start()
+    for copy in copies:
+        copy.wait()
+
+
+def finish(latent, total):
+    anywhere = pl.BlockSpec(memory_space=pl.ANY)
+    shapes = [(SPEC, C), (C, C), (C, C), (9, C)]
+    return pl.pallas_call(
+        finish_kernel,
+        out_shape=[jax.ShapeDtypeStruct((CELLS, C), bf16)]
+        + [jax.ShapeDtypeStruct(shape, f32) for shape in shapes],
+        in_specs=[anywhere, anywhere],
+        out_specs=[anywhere] * 4 + [vmem()],
+        scratch_shapes=[VMEM((PARTS, C), bf16)]
+        + [VMEM(shape, f32) for shape in shapes[:3]]
+        + [VMEM((CELLS, C), bf16), pltpu.SemaphoreType.DMA((8,))],
+        compiler_params=pltpu.CompilerParams(vmem_limit_bytes=62 << 20),
+    )(latent, total)
 
 
 def on_device(spectra, owner, cell, w_in, w_out, w_point, w_depth, cotangent):
-    zero = jnp.zeros((13, OBS), bf16)
-    rows = jnp.concatenate(
-        [jnp.stack([owner[:, 0], cell // 16, cell % 16]).astype(bf16), zero], axis=0
+    latent, total = run(
+        spectra.T,
+        owner.reshape(1, OBS),
+        cell.reshape(1, OBS),
+        w_in,
+        w_out,
+        w_point,
+        w_depth,
+        cotangent.reshape(CELLS, C),
     )
-    latent, total = run(
-        spectra.T, rows, w_in, w_out, w_point, w_depth, cotangent.reshape(CELLS, C)
-    )
-    total = total.astype(f32)
-    tiles = N_LAT * N_LON
-    obs_scale = 1.0 / jnp.sqrt(f32(OBS * tiles))
-    cell_scale = 1.0 / jnp.sqrt(f32(CELLS * tiles))
-    at = ROWS_IN
-    late = LATE.first
-    return (
-        latent.reshape(CLAT, CLON, C),
-        total[:SPEC] * obs_scale,
-        total[at : at + C] * obs_scale,
-        total[late : late + C] * cell_scale,
-        total[late + C : late + C + 9] * cell_scale,
-    )
+    latent, *grads = finish(latent, total)
+    return (latent.reshape(CLAT, CLON, C), *grads)
 
 
 def solution(mesh):

time: 106 us -> 91.6 us (0.86)
  other arithmetic: 7.28 us -> 0 us
  Pallas kernels: 95.9 us -> 90.8 us
  local copies, waits for them, and re-layouts: 1.51 us -> 0 us
    pallas_call x1, Pallas kernels: 95.9 us -> 86.5 us  [run(): pl.pallas_call(kernel, out_shape=[jax.ShapeDtypeStruct((CELLS, C), bf16),...]
    pallas_call x0 -> x1, Pallas kernels: none -> 4.28 us  [finish(): pl.pallas_call(finish_kernel, out_shape=[jax.ShapeDtypeStruct((CELLS, C),...]
    mul x3 -> x0, other arithmetic: 3.33 us -> none  [the longest x1 1.55 us: on_device(): total[late:late + C] * cell_scale]
    another operation x3 -> x0, other arithmetic: 2 us -> none  [the longest x2 1.31 us: on_device(): jnp.stack([owner[:, 0], cell // 16, cell % 16]).astype(bf16)]
    convert_element_type x1 -> x0, other arithmetic: 1.94 us -> none  [on_device(): total = total.astype(f32)]
    unnamed x3 -> x0, local copies, waits for them, and re-layouts: 1.5 us -> none
where the time goes in v3:
time: 91.6 us; the launch traced here: 91.4 us
  Pallas kernels  90.8 us (99%)
    pallas_call x1, Pallas kernels, run(): pl.pallas_call(kernel, out_shape=[jax.ShapeDtypeStruct((CELLS, C), bf16),...  86.5 us
    pallas_call x1, Pallas kernels, finish(): pl.pallas_call(finish_kernel, out_shape=[jax.ShapeDtypeStruct((CELLS, C),...  4.28 us

profile of v3, /device:TPU:1, one launch (start us, length us, event | category | flops | bytes accessed | tf_op | source)
XLA Modules:
  0.0 91.4 jit_solution(3141688931634887688)
XLA Ops:
  0.6 86.5 %shard_map.119 = (bf16[2048,512]{1,0:T(8,128)(2,1)}, bf16[1664,512]{1,0:T(8,128)(2,1)}) custom-call(bf16[616,512]{1,0:T(8,128)(2,1)} %bitcast.6, s32[1,512]{1,0:T(1,128)} %bitcast.7, s32[1,512]{1,0:T(1,128)} %bitcast.8, bf16[616,512]{1,0:T(8,128)(2,1)} %w_in_in.1, bf16[512,512]{1,0:T(8,128)(2,1)} %w_out_in.1, bf16[512,512]{1,0:T(8,128)(2,1)} %w_point_in.1, ...), custom_call_target="tpu_custom_call" | custom-call | tf_op jit(solution)/shard_map/pallas_call | solution.py:730
  87.2 4.3 %shard_map.120 = (bf16[2048,512]{1,0:T(8,128)(2,1)}, f32[616,512]{1,0:T(8,128)}, f32[512,512]{1,0:T(8,128)}, f32[512,512]{1,0:T(8,128)}, f32[9,512]{1,0:T(8,128)}) custom-call(bf16[2048,512]{1,0:T(8,128)(2,1)} %get-tuple-element.12.latent_in, bf16[1664,512]{1,0:T(8,128)(2,1)} %get-tuple-element.13.total_in), custom_call_target="tpu_custom_call" | custom-call | tf_op jit(solution)/shard_map/pallas_call | solution.py:833

commit v4 on v3

--- a/solution.py
+++ b/solution.py
@@ -257,15 +257,13 @@
             sides[side, i, 0:1, :] = total[i : i + 1, :]
 
 
-def conv_part(rows, sides, i, lanes, weight):
+def conv_part(rows, first, last, weight):
     columns = [
         weight(b) * rows[0] + weight(3 + b) * rows[1] + weight(6 + b) * rows[2] for b in range(3)
     ]
     index = lax.broadcasted_iota(i32, (CLON, CHUNK), 0)
-    left = jnp.where(index == 0, sides[0, i, 0:1, lanes], pltpu.roll(columns[0], 1, 0))
-    right = jnp.where(
-        index == CLON - 1, sides[1, i, 0:1, lanes], pltpu.roll(columns[2], CLON - 1, 0)
-    )
+    left = jnp.where(index == 0, first, pltpu.roll(columns[0], 1, 0))
+    right = jnp.where(index == CLON - 1, last, pltpu.roll(columns[2], CLON - 1, 0))
     return columns[1] + left + right
 
 
@@ -279,7 +277,7 @@
     w_depth,
     cot_in,
     latent,
-    result,
+    sums_out,
     spec_t,
     w_in,
     w_out,
@@ -309,6 +307,8 @@
     west,
     east,
     sides,
+    ends,
+    depth_sums,
     g_grid,
     g_arrived,
     returned,
@@ -330,6 +330,8 @@
     gather_out,
     gather_point,
     latent_here,
+    result,
+    out_sem,
     load_sem,
     local_sem,
     send_sem,
@@ -442,7 +444,8 @@
         for chunk in range(C // CHUNK):
             lanes = slice(chunk * CHUNK, (chunk + 1) * CHUNK)
             three = [gm_ext[i + a, :, lanes].astype(f32) for a in range(3)]
-            acc = conv_part(three, sides, i, lanes, lambda k: w_depth[8 - k : 9 - k, lanes])
+            first, last = sides[0, i, 0:1, lanes], sides[1, i, 0:1, lanes]
+            acc = conv_part(three, first, last, lambda k: w_depth[8 - k : 9 - k, lanes])
             at = pl.ds(pl.multiple_of(i * CLON, CLON), CLON)
             g_grid[at, lanes] = (cot[at, lanes].astype(f32) + acc).astype(bf16)
         return carry
@@ -503,17 +506,17 @@
     edge_columns(grid_ext, cols_f.at[pl.ds(2, 2)])
     cols_x[...] = cols_f[2:4].astype(bf16)
     halo_x.start()
-    halo_x.wait()
-    side_columns(to_cols_x, to_diag_x, west, east)
-    side_sums(west, east, lambda k: w_depth[k : k + 1, :], sides)
-    for chunk in range(C // CHUNK):
+
+    def conv_rows(low, high, chunk, sums):
         lanes = slice(chunk * CHUNK, (chunk + 1) * CHUNK)
 
-        def conv_forward(i, sums, lanes=lanes):
+        def one(i, sums):
             three = [grid_ext[i + a, :, lanes].astype(f32) for a in range(3)]
-            acc = conv_part(three, sides, i, lanes, lambda k: w_depth[k : k + 1, lanes])
+            acc = conv_part(three, 0.0, 0.0, lambda k: w_depth[k : k + 1, lanes])
             at = pl.ds(pl.multiple_of(i * CLON, CLON), CLON)
             mixed[at, lanes] = acc.astype(bf16)
+            ends[0, i, 0:1, lanes] = acc[0:1]
+            ends[1, i, 0:1, lanes] = acc[CLON - 1 : CLON]
             middle = gm_ext[i + 1, :, lanes].astype(f32)
             index = lax.broadcasted_iota(i32, (CLON, CHUNK), 0)
             shifted = [
@@ -527,7 +530,19 @@
                 for b in range(3)
             )
 
-        sums = lax.fori_loop(0, CLAT, conv_forward, tuple(jnp.zeros((8, CHUNK), f32) for _ in range(9)))
+        return lax.fori_loop(low, high, one, sums)
+
+    for chunk in range(C // CHUNK):
+        sums = conv_rows(1, CLAT - 1, chunk, tuple(jnp.zeros((8, CHUNK), f32) for _ in range(9)))
+        for k in range(9):
+            depth_sums[chunk, k] = sums[k]
+    halo_x.wait()
+    side_columns(to_cols_x, to_diag_x, west, east)
+    side_sums(west, east, lambda k: w_depth[k : k + 1, :], sides)
+    for chunk in range(C // CHUNK):
+        lanes = slice(chunk * CHUNK, (chunk + 1) * CHUNK)
+        sums = conv_rows(0, 1, chunk, tuple(depth_sums[chunk, k] for k in range(9)))
+        sums = conv_rows(CLAT - 1, CLAT, chunk, sums)
         for k, (a, b) in enumerate(offsets):
             total = jnp.sum(sums[k], axis=0, keepdims=True)
             if b:
@@ -535,6 +550,17 @@
                 edge = cols_f[0 if b < 0 else 1, :, lanes].astype(bf16).astype(f32)
                 total = total + jnp.sum(side * edge, axis=0, keepdims=True)
             parts[DEPTH + k : DEPTH + k + 1, lanes] = total
+
+    def side_rows(i, carry):
+        index = lax.broadcasted_iota(i32, (16, C), 0)
+        for side, row in ((0, 0), (1, CLON - 16)):
+            at = pl.ds(pl.multiple_of(i * CLON + row, 16), 16)
+            whole = (ends[side, i, 0:1, :] + sides[side, i, 0:1, :]).astype(bf16).astype(f32)
+            old = mixed[at, :].astype(f32)
+            mixed[at, :] = jnp.where(index == 15 * side, whole, old).astype(bf16)
+        return carry
+
+    lax.fori_loop(0, CLAT, side_rows, 0)
     parts[SPEC:DEPTH, :] = jnp.zeros((DEPTH - SPEC, C), f32)
     parts[DEPTH + 9 : ROWS_IN, :] = jnp.zeros((ROWS_IN - DEPTH - 9, C), f32)
     parts[POINT.first : PARTS, :] = dot(mixed[...], cot[...], ((0,), (0,)))
@@ -712,13 +738,27 @@
     point(3)
     store = pltpu.make_async_copy(latent_here, latent, local_sem.at[6])
     store.start()
-    last = [last_swap(POINT), last_swap(OUT), last_swap(IN)]
-    for r in (POINT, OUT, IN):
+    rounds = (POINT, OUT, IN)
+
+    def leave(r, which, index):
+        half = half_of(r, which)
+        return pltpu.make_async_copy(result.at[half], sums_out.at[half], out_sem.at[index])
+
+    last, leaving = [], []
+    for i, r in enumerate(rounds):
+        last.append(last_swap(r))
+        leaving.append(leave(r, core, i))
+        leaving[-1].start()
+    for r in rounds:
         sent(r)
     store.wait()
     for copy in (lat_marks, lon_marks, all_data, all_back):
         copy.wait_send()
-    for copy in last:
+    for i, r in enumerate(rounds):
+        last[i].wait()
+        leaving.append(leave(r, 1 - core, 3 + i))
+        leaving[-1].start()
+    for copy in leaving:
         copy.wait()
 
 
@@ -730,11 +770,11 @@
     return pl.pallas_call(
         kernel,
         out_shape=[
-            jax.ShapeDtypeStruct((CELLS, C), bf16),
-            jax.ShapeDtypeStruct((PARTS, C), bf16),
+            pltpu.VMEM((CELLS, C), bf16),
+            pltpu.VMEM((PARTS, C), bf16),
         ],
         in_specs=[anywhere, vmem(), vmem(), anywhere, anywhere, anywhere, vmem(), anywhere],
-        out_specs=[anywhere, vmem()],
+        out_specs=[anywhere, anywhere],
         scratch_shapes=[
             VMEM((SPEC, OBS), bf16),
             VMEM((SPEC, C), bf16),
@@ -765,6 +805,8 @@
             VMEM((24, C), f32),
             VMEM((24, C), f32),
             VMEM((2, CLAT, 8, C), f32),
+            VMEM((2, CLAT, 8, C), f32),
+            VMEM((C // CHUNK, 9, 8, CHUNK), f32),
             VMEM((CELLS, C), bf16),
             VMEM((SLOTS, C), bf16),
             VMEM((SLOTS, C), bf16),
@@ -782,6 +824,8 @@
         + [VMEM((16, 16, r.width), bf16) for r in (IN, OUT, POINT)]
         + [
             VMEM((CELLS, C), bf16),
+            VMEM((PARTS, C), bf16),
+            dma((6,)),
             dma((5,)),
             dma((7,)),
             dma((SEMS,)),
@@ -790,39 +834,26 @@
             dma((2, 8)),
         ],
         compiler_params=pltpu.CompilerParams(
-            collective_id=0, has_side_effects=True, vmem_limit_bytes=60 << 20
+            collective_id=0, has_side_effects=True, vmem_limit_bytes=51 << 20
         ),
     )(spec_t, owner, cell, w_in, w_out, w_point, w_depth, cot)
 
 
-def finish_kernel(
-    latent_in, total_in, latent, g_in, g_out, g_point, g_depth, total, in_f, out_f, point_f, latent_here, sem
-):
+def finish_kernel(latent_in, total, latent, g_in, g_out, g_point, g_depth, in_f, out_f, point_f, sem):
     obs_scale = 1.0 / math.sqrt(OBS * N_LAT * N_LON)
     cell_scale = 1.0 / math.sqrt(CELLS * N_LAT * N_LON)
+    copies = [pltpu.make_async_copy(latent_in, latent, sem.at[3])]
+    copies[0].start()
     plan = (
-        (in_f, g_in, IN.first, 640, obs_scale),
-        (out_f, g_out, OUT.first, C, obs_scale),
-        (point_f, g_point, POINT.first, C, cell_scale),
+        (in_f, g_in, IN.first, obs_scale),
+        (out_f, g_out, OUT.first, obs_scale),
+        (point_f, g_point, POINT.first, cell_scale),
     )
-    loads = []
-    for i, (_, _, first, size, _) in enumerate(plan):
-        rows = pl.ds(first, size)
-        loads.append(pltpu.make_async_copy(total_in.at[rows], total.at[rows], sem.at[i]))
-    loads.append(pltpu.make_async_copy(latent_in, latent_here, sem.at[3]))
-    for copy in loads:
-        copy.start()
-    copies = []
-    for i, (values, target, first, _, scale) in enumerate(plan):
-        loads[i].wait()
+    for i, (values, target, first, scale) in enumerate(plan):
         values[...] = total[first : first + values.shape[0], :].astype(f32) * scale
-        copies.append(pltpu.make_async_copy(values, target, sem.at[4 + i]))
+        copies.append(pltpu.make_async_copy(values, target, sem.at[i]))
         copies[-1].start()
-        if i == 0:
-            g_depth[...] = total[DEPTH : DEPTH + 16, :].astype(f32)[0:9] * cell_scale
-    loads[3].wait()
-    copies.append(pltpu.make_async_copy(latent_here, latent, sem.at[7]))
-    copies[-1].start()
+    g_depth[...] = total[DEPTH : DEPTH + 16, :].astype(f32)[0:9] * cell_scale
     for copy in copies:
         copy.wait()
 
@@ -834,12 +865,10 @@
         finish_kernel,
         out_shape=[jax.ShapeDtypeStruct((CELLS, C), bf16)]
         + [jax.ShapeDtypeStruct(shape, f32) for shape in shapes],
-        in_specs=[anywhere, anywhere],
+        in_specs=[vmem(), vmem()],
         out_specs=[anywhere] * 4 + [vmem()],
-        scratch_shapes=[VMEM((PARTS, C), bf16)]
-        + [VMEM(shape, f32) for shape in shapes[:3]]
-        + [VMEM((CELLS, C), bf16), pltpu.SemaphoreType.DMA((8,))],
-        compiler_params=pltpu.CompilerParams(vmem_limit_bytes=62 << 20),
+        scratch_shapes=[VMEM(shape, f32) for shape in shapes[:3]] + [pltpu.SemaphoreType.DMA((4,))],
+        compiler_params=pltpu.CompilerParams(vmem_limit_bytes=12 << 20),
     )(latent, total)
 
 

time: 91.6 us -> 86.7 us (0.947)
  Pallas kernels: 90.8 us -> 85.9 us
    pallas_call x1, Pallas kernels: 86.5 us -> 82.8 us  [run(): pl.pallas_call(kernel, out_shape=[pltpu.VMEM((CELLS, C), bf16), pltpu.VME...]
    pallas_call x1, Pallas kernels: 4.28 us -> 3.07 us  [finish(): pl.pallas_call(finish_kernel, out_shape=[jax.ShapeDtypeStruct((CELLS, C),...]
where the time goes in v4:
time: 86.7 us; the launch traced here: 86.5 us
  Pallas kernels  85.9 us (99%)
    pallas_call x1, Pallas kernels, run(): pl.pallas_call(kernel, out_shape=[pltpu.VMEM((CELLS, C), bf16), pltpu.VME...  82.8 us
    pallas_call x1, Pallas kernels, finish(): pl.pallas_call(finish_kernel, out_shape=[jax.ShapeDtypeStruct((CELLS, C),...  3.07 us

profile of v4, /device:TPU:1, one launch (start us, length us, event | category | flops | bytes accessed | tf_op | source)
XLA Modules:
  0.0 86.5 jit_solution(13925768655687571416)
XLA Ops:
  0.6 82.8 %shard_map.119 = (bf16[2048,512]{1,0:T(8,128)(2,1)S(1)}, bf16[1664,512]{1,0:T(8,128)(2,1)S(1)}) custom-call(bf16[616,512]{1,0:T(8,128)(2,1)} %bitcast.6, s32[1,512]{1,0:T(1,128)} %bitcast.7, s32[1,512]{1,0:T(1,128)} %bitcast.8, bf16[616,512]{1,0:T(8,128)(2,1)} %w_in_in.1, bf16[512,512]{1,0:T(8,128)(2,1)} %w_out_in.1, bf16[512,512]{1,0:T(8,128)(2,1)} %w_point_in.1, ...), custom_call_target="tpu_custom_call" | custom-call | tf_op jit(solution)/shard_map/pallas_call | solution.py:770
  83.4 3.1 %shard_map.120 = (bf16[2048,512]{1,0:T(8,128)(2,1)}, f32[616,512]{1,0:T(8,128)}, f32[512,512]{1,0:T(8,128)}, f32[512,512]{1,0:T(8,128)}, f32[9,512]{1,0:T(8,128)}) custom-call(bf16[2048,512]{1,0:T(8,128)(2,1)S(1)} %get-tuple-element.12.latent_in, bf16[1664,512]{1,0:T(8,128)(2,1)S(1)} %get-tuple-element.13.total), custom_call_target="tpu_custom_call" | custom-call | tf_op jit(solution)/shard_map/pallas_call | solution.py:864

commit v5 on v4

--- a/solution.py
+++ b/solution.py
@@ -232,10 +232,16 @@
     return ref.at[pl.ds(pl.multiple_of(chip * size, size), size)]
 
 
-def edge_columns(ext, cols):
-    for side, (at, row) in enumerate(((0, 0), (CLON - 16, 15))):
-        for i in range(CLAT):
-            cols[side, i : i + 1, :] = ext[1 + i, at : at + 16, :].astype(f32)[row : row + 1]
+def keep_ends(ends, row, values):
+    for r in range(values.shape[0] // CLON):
+        at = r * CLON
+        ends[0, row + r, 0:1, :] = values[at : at + 1]
+        ends[1, row + r, 0:1, :] = values[at + CLON - 1 : at + CLON]
+
+
+def edge_columns(ends, cols):
+    for side in range(2):
+        cols[side] = ends[side, :, 0, :].astype(bf16)
 
 
 def side_columns(to_cols, to_diag, west, east):
@@ -297,7 +303,6 @@
     places,
     gm_ext,
     grid_ext,
-    cols_f,
     cols,
     to_cols,
     to_diag,
@@ -367,18 +372,6 @@
     for copy in loads[:3]:
         copy.wait()
     vector_encode(spec_t, owner, cell, w_in, w_out, preact, hidden, emb, route, table)
-    for copy in loads[3:]:
-        copy.wait()
-
-    def mix_back(i, carry):
-        rows4 = cot[pl.ds(pl.multiple_of(i * 512, 512), 512), :]
-        gm = dot(rows4, w_point[...], ((1,), (1,))).astype(bf16)
-        gm_ext[pl.ds(1 + 4 * i, 4)] = gm.reshape(4, CLON, C)
-        return carry
-
-    lax.fori_loop(0, CLAT // 4, mix_back, 0)
-    edge_columns(gm_ext, cols_f.at[pl.ds(0, 2)])
-    cols[...] = cols_f[0:2].astype(bf16)
     pl.semaphore_wait(barrier, count)
 
     swaps = [
@@ -394,8 +387,6 @@
     for step in range(1, N_LAT):
         lat = (place.lat + step) % N_LAT
         cross(table.at[lat], table_lat.at[place.lat], MARK_LAT, (lat, place.lon)).start()
-    halo_g.start()
-
     def spread(key, values, more):
         def one(i, carry):
             at = pl.multiple_of(i * PART, PART)
@@ -410,6 +401,19 @@
         lax.fori_loop(0, SLOTS // PART, one, 0)
 
     spread(slot_keys(route[...], core, core), emb, False)
+    for copy in loads[3:]:
+        copy.wait()
+
+    def mix_back(i, carry):
+        rows4 = cot[pl.ds(pl.multiple_of(i * 512, 512), 512), :]
+        gm = dot(rows4, w_point[...], ((1,), (1,)))
+        gm_ext[pl.ds(1 + 4 * i, 4)] = gm.astype(bf16).reshape(4, CLON, C)
+        keep_ends(ends, 4 * i, gm)
+        return carry
+
+    lax.fori_loop(0, CLAT // 4, mix_back, 0)
+    edge_columns(ends, cols)
+    halo_g.start()
     keep_lat.wait()
     lat_row = pl.ds(0, N_LAT - 1)
     lat_marks = cross(table.at[lat_row], table_lat.at[lat_row], MARK_LAT, place.sibling)
@@ -498,13 +502,13 @@
     def bin_rows(i, carry):
         index = lax.broadcasted_iota(i32, (PART, SLOTS), 0) + i * PART
         pick = (index == place_row).astype(f32).astype(bf16)
-        cells_here = dot(pick, arrived[...], ((1,), (0,))).astype(bf16)
-        grid_ext[pl.ds(1 + 2 * i, 2)] = cells_here.reshape(2, CLON, C)
+        cells_here = dot(pick, arrived[...], ((1,), (0,)))
+        grid_ext[pl.ds(1 + 2 * i, 2)] = cells_here.astype(bf16).reshape(2, CLON, C)
+        keep_ends(ends, 2 * i, cells_here)
         return carry
 
     lax.fori_loop(0, CELLS // PART, bin_rows, 0)
-    edge_columns(grid_ext, cols_f.at[pl.ds(2, 2)])
-    cols_x[...] = cols_f[2:4].astype(bf16)
+    edge_columns(ends, cols_x)
     halo_x.start()
 
     def conv_rows(low, high, chunk, sums):
@@ -547,7 +551,7 @@
             total = jnp.sum(sums[k], axis=0, keepdims=True)
             if b:
                 side = (west if b < 0 else east)[1 + a : 1 + a + CLAT, lanes]
-                edge = cols_f[0 if b < 0 else 1, :, lanes].astype(bf16).astype(f32)
+                edge = cols[0 if b < 0 else 1, :, lanes].astype(f32)
                 total = total + jnp.sum(side * edge, axis=0, keepdims=True)
             parts[DEPTH + k : DEPTH + k + 1, lanes] = total
 
@@ -563,7 +567,6 @@
     lax.fori_loop(0, CLAT, side_rows, 0)
     parts[SPEC:DEPTH, :] = jnp.zeros((DEPTH - SPEC, C), f32)
     parts[DEPTH + 9 : ROWS_IN, :] = jnp.zeros((ROWS_IN - DEPTH - 9, C), f32)
-    parts[POINT.first : PARTS, :] = dot(mixed[...], cot[...], ((0,), (0,)))
 
     lines = {IN: lines_in, OUT: lines_out, POINT: lines_point}
     quarter = {IN: quarter_in, OUT: quarter_out, POINT: quarter_point}
@@ -689,7 +692,6 @@
         here = grid_ext[1 + 4 * i : 5 + 4 * i].astype(f32).reshape(512, C)
         latent_here[at, :] = (here + dot(mixed[at, :], w_point[...], ((1,), (0,)))).astype(bf16)
 
-    point_swap = swap_halves(POINT)
 
     keep_back.wait()
     all_back = cross(g_arrived.at[some], returned.at[some], BACK, place.sibling)
@@ -706,6 +708,8 @@
     part[...] = gathered(slot_keys(route_sib[...], core, 1 - core)).astype(bf16)
     swap = cross(part, part_sib, SIB_PART, place.sibling)
     swap.start()
+    parts[POINT.first : PARTS, :] = dot(mixed[...], cot[...], ((0,), (0,)))
+    point_swap = swap_halves(POINT)
     own = gathered(slot_keys(route[...], core, core))
     swap.wait()
     g_emb[...] = (own + part_sib[...].astype(f32)).astype(bf16)
@@ -795,7 +799,6 @@
             VMEM((N_LON, N_LAT, META), f32),
             field,
             field,
-            VMEM((4, CLAT, C), f32),
             VMEM((2, CLAT, C), bf16),
             VMEM((2, CLAT, C), bf16),
             VMEM((4, CLAT, C), bf16),

time: 86.7 us -> 82.5 us (0.952)
  Pallas kernels: 85.9 us -> 81.7 us
    pallas_call x1, Pallas kernels: 82.8 us -> 78.6 us  [run(): pl.pallas_call(kernel, out_shape=[pltpu.VMEM((CELLS, C), bf16), pltpu.VME...]
where the time goes in v5:
time: 82.5 us; the launch traced here: 82.3 us
  Pallas kernels  81.7 us (99%)
    pallas_call x1, Pallas kernels, run(): pl.pallas_call(kernel, out_shape=[pltpu.VMEM((CELLS, C), bf16), pltpu.VME...  78.6 us
    pallas_call x1, Pallas kernels, finish(): pl.pallas_call(finish_kernel, out_shape=[jax.ShapeDtypeStruct((CELLS, C),...  3.07 us

profile of v5, /device:TPU:1, one launch (start us, length us, event | category | flops | bytes accessed | tf_op | source)
XLA Modules:
  0.0 82.3 jit_solution(17567194828011435535)
XLA Ops:
  0.6 78.6 %shard_map.119 = (bf16[2048,512]{1,0:T(8,128)(2,1)S(1)}, bf16[1664,512]{1,0:T(8,128)(2,1)S(1)}) custom-call(bf16[616,512]{1,0:T(8,128)(2,1)} %bitcast.6, s32[1,512]{1,0:T(1,128)} %bitcast.7, s32[1,512]{1,0:T(1,128)} %bitcast.8, bf16[616,512]{1,0:T(8,128)(2,1)} %w_in_in.1, bf16[512,512]{1,0:T(8,128)(2,1)} %w_out_in.1, bf16[512,512]{1,0:T(8,128)(2,1)} %w_point_in.1, ...), custom_call_target="tpu_custom_call" | custom-call | tf_op jit(solution)/shard_map/pallas_call | solution.py:774
  79.3 3.1 %shard_map.120 = (bf16[2048,512]{1,0:T(8,128)(2,1)}, f32[616,512]{1,0:T(8,128)}, f32[512,512]{1,0:T(8,128)}, f32[512,512]{1,0:T(8,128)}, f32[9,512]{1,0:T(8,128)}) custom-call(bf16[2048,512]{1,0:T(8,128)(2,1)S(1)} %get-tuple-element.12.latent_in, bf16[1664,512]{1,0:T(8,128)(2,1)S(1)} %get-tuple-element.13.total), custom_call_target="tpu_custom_call" | custom-call | tf_op jit(solution)/shard_map/pallas_call | solution.py:867

commit v6 on v5

--- a/solution.py
+++ b/solution.py
@@ -178,7 +178,12 @@
     kind = lane // CAP
     value = jnp.where(kind == 0, high_col, jnp.where(kind == 1, low_col, 1.0))
     keep = (lane % CAP == pos_col) & (kind < 3)
-    emb[:, C:] = jnp.where(keep, value, 0.0).astype(bf16)
+    tile_at = tile_col.astype(i32)
+    lat_at = tile_at // N_LON
+    chip_at = lat_at // 2 * N_LON + tile_at % N_LON
+    about = jnp.where(lane == 24, chip_at, jnp.where(lane == 25, pos_col, lat_at % 2)).astype(f32)
+    about = jnp.where((lane >= 24) & (lane < 27), about, 0.0)
+    emb[:, C:] = jnp.where(keep, value, about).astype(bf16)
     table[...] = dot(hits_t.astype(bf16), emb[:, C:], ((1,), (0,))).reshape(N_LAT, N_LON, META)
     tile = tile_row.astype(i32)
     lat, lon = tile // N_LON, tile % N_LON
@@ -251,14 +256,17 @@
         into[CLAT + 1 : CLAT + 2, :] = to_diag[below].astype(f32)[0:1]
 
 
+def side_totals(west, east, weight):
+    return [
+        weight(b) * ref[0:CLAT, :]
+        + weight(3 + b) * ref[1 : CLAT + 1, :]
+        + weight(6 + b) * ref[2 : CLAT + 2, :]
+        for b, ref in ((0, west), (2, east))
+    ]
+
+
 def side_sums(west, east, weight, sides):
-    for side, ref in ((0, west), (1, east)):
-        b = 2 * side
-        total = (
-            weight(b) * ref[0:CLAT, :]
-            + weight(3 + b) * ref[1 : CLAT + 1, :]
-            + weight(6 + b) * ref[2 : CLAT + 2, :]
-        )
+    for side, total in enumerate(side_totals(west, east, weight)):
         for i in range(CLAT):
             sides[side, i, 0:1, :] = total[i : i + 1, :]
 
@@ -477,7 +485,7 @@
         else:
             wide = dot(known, expand, ((0,), (0,)))
         value = jnp.where(other < CAP, 16.0, 1.0) * wide
-        keep = jnp.where(other % CAP == slot % CAP, value, 0.0)
+        keep = jnp.where((other % CAP == slot % CAP) & (other < 3 * CAP), value, 0.0)
         return (jnp.sum(keep, axis=1 - axis, keepdims=True) - 1.0).astype(i32)
 
     place_col, place_row = cells_of(0), cells_of(1)
@@ -542,7 +550,6 @@
             depth_sums[chunk, k] = sums[k]
     halo_x.wait()
     side_columns(to_cols_x, to_diag_x, west, east)
-    side_sums(west, east, lambda k: w_depth[k : k + 1, :], sides)
     for chunk in range(C // CHUNK):
         lanes = slice(chunk * CHUNK, (chunk + 1) * CHUNK)
         sums = conv_rows(0, 1, chunk, tuple(depth_sums[chunk, k] for k in range(9)))
@@ -555,16 +562,13 @@
                 total = total + jnp.sum(side * edge, axis=0, keepdims=True)
             parts[DEPTH + k : DEPTH + k + 1, lanes] = total
 
-    def side_rows(i, carry):
-        index = lax.broadcasted_iota(i32, (16, C), 0)
-        for side, row in ((0, 0), (1, CLON - 16)):
-            at = pl.ds(pl.multiple_of(i * CLON + row, 16), 16)
-            whole = (ends[side, i, 0:1, :] + sides[side, i, 0:1, :]).astype(bf16).astype(f32)
-            old = mixed[at, :].astype(f32)
-            mixed[at, :] = jnp.where(index == 15 * side, whole, old).astype(bf16)
-        return carry
-
-    lax.fori_loop(0, CLAT, side_rows, 0)
+    index = lax.broadcasted_iota(i32, (16, C), 0)
+    for side, beside in enumerate(side_totals(west, east, lambda k: w_depth[k : k + 1, :])):
+        for i in range(CLAT):
+            at = i * CLON + side * (CLON - 16)
+            whole = (ends[side, i, 0:1, :] + beside[i : i + 1]).astype(bf16).astype(f32)
+            old = mixed[at : at + 16, :].astype(f32)
+            mixed[at : at + 16, :] = jnp.where(index == 15 * side, whole, old).astype(bf16)
     parts[SPEC:DEPTH, :] = jnp.zeros((DEPTH - SPEC, C), f32)
     parts[DEPTH + 9 : ROWS_IN, :] = jnp.zeros((ROWS_IN - DEPTH - 9, C), f32)
 
@@ -697,20 +701,23 @@
     all_back = cross(g_arrived.at[some], returned.at[some], BACK, place.sibling)
     all_back.wait_recv()
 
-    def gathered(key):
+    def gathered(info, which):
+        about = info[:, C:].astype(f32)
+        slot = about[:, 24:25] * SLOT + about[:, 25:26] + (CAP * which).astype(f32)
+        key = jnp.where(about[:, 26:27] == core.astype(f32), slot, -1.0)
         total = jnp.zeros((OBS, C), f32)
-        for at in range(0, SLOTS, PART):
-            index = lax.broadcasted_iota(i32, (PART, OBS), 0) + at
+        for at in range(0, SLOTS, 512):
+            index = (lax.broadcasted_iota(i32, (OBS, 512), 1) + at).astype(f32)
             pick = (index == key).astype(f32).astype(bf16)
-            total = total + dot(pick, returned[at : at + PART, :], ((0,), (0,)))
+            total = total + dot(pick, returned[at : at + 512, :], ((1,), (0,)))
         return total
 
-    part[...] = gathered(slot_keys(route_sib[...], core, 1 - core)).astype(bf16)
+    part[...] = gathered(emb_sib, 1 - core).astype(bf16)
     swap = cross(part, part_sib, SIB_PART, place.sibling)
     swap.start()
     parts[POINT.first : PARTS, :] = dot(mixed[...], cot[...], ((0,), (0,)))
     point_swap = swap_halves(POINT)
-    own = gathered(slot_keys(route[...], core, core))
+    own = gathered(emb, core)
     swap.wait()
     g_emb[...] = (own + part_sib[...].astype(f32)).astype(bf16)
     parts[OUT.first : OUT.first + C, :] = dot(hidden[...], g_emb[...], ((0,), (0,)))

time: 82.5 us -> 82.9 us (level)
  no operation moved by 1% of the time
where the time goes in v6:
time: 82.9 us; the launch traced here: 82.7 us
  Pallas kernels  82.1 us (99%)
    pallas_call x1, Pallas kernels, run(): pl.pallas_call(kernel, out_shape=[pltpu.VMEM((CELLS, C), bf16), pltpu.VME...  79 us
    pallas_call x1, Pallas kernels, finish(): pl.pallas_call(finish_kernel, out_shape=[jax.ShapeDtypeStruct((CELLS, C),...  3.07 us

profile of v6, /device:TPU:1, one launch (start us, length us, event | category | flops | bytes accessed | tf_op | source)
XLA Modules:
  0.0 82.7 jit_solution(10809157370885121568)
XLA Ops:
  0.6 79.0 %shard_map.119 = (bf16[2048,512]{1,0:T(8,128)(2,1)S(1)}, bf16[1664,512]{1,0:T(8,128)(2,1)S(1)}) custom-call(bf16[616,512]{1,0:T(8,128)(2,1)} %bitcast.6, s32[1,512]{1,0:T(1,128)} %bitcast.7, s32[1,512]{1,0:T(1,128)} %bitcast.8, bf16[616,512]{1,0:T(8,128)(2,1)} %w_in_in.1, bf16[512,512]{1,0:T(8,128)(2,1)} %w_out_in.1, bf16[512,512]{1,0:T(8,128)(2,1)} %w_point_in.1, ...), custom_call_target="tpu_custom_call" | custom-call | tf_op jit(solution)/shard_map/pallas_call | solution.py:781
  79.6 3.1 %shard_map.120 = (bf16[2048,512]{1,0:T(8,128)(2,1)}, f32[616,512]{1,0:T(8,128)}, f32[512,512]{1,0:T(8,128)}, f32[512,512]{1,0:T(8,128)}, f32[9,512]{1,0:T(8,128)}) custom-call(bf16[2048,512]{1,0:T(8,128)(2,1)S(1)} %get-tuple-element.12.latent_in, bf16[1664,512]{1,0:T(8,128)(2,1)S(1)} %get-tuple-element.13.total), custom_call_target="tpu_custom_call" | custom-call | tf_op jit(solution)/shard_map/pallas_call | solution.py:874

commit v7 on v5

--- a/solution.py
+++ b/solution.py
@@ -358,7 +358,7 @@
             )
         )
     ]
-    for copy in loads:
+    for copy in loads[:3]:
         copy.start()
     barrier, count = greet(place)
 
@@ -371,6 +371,8 @@
     halo_x.clear_outside()
     for copy in loads[:3]:
         copy.wait()
+    for copy in loads[3:]:
+        copy.start()
     vector_encode(spec_t, owner, cell, w_in, w_out, preact, hidden, emb, route, table)
     pl.semaphore_wait(barrier, count)
 

time: 82.5 us -> 82.5 us (level)
  no operation moved by 1% of the time
where the time goes in v7:
time: 82.5 us; the launch traced here: 82.3 us
  Pallas kernels  81.6 us (99%)
    pallas_call x1, Pallas kernels, run(): pl.pallas_call(kernel, out_shape=[pltpu.VMEM((CELLS, C), bf16), pltpu.VME...  78.6 us
    pallas_call x1, Pallas kernels, finish(): pl.pallas_call(finish_kernel, out_shape=[jax.ShapeDtypeStruct((CELLS, C),...  3.07 us

profile of v7, /device:TPU:1, one launch (start us, length us, event | category | flops | bytes accessed | tf_op | source)
XLA Modules:
  0.0 82.3 jit_solution(7448526044470771977)
XLA Ops:
  0.6 78.6 %shard_map.119 = (bf16[2048,512]{1,0:T(8,128)(2,1)S(1)}, bf16[1664,512]{1,0:T(8,128)(2,1)S(1)}) custom-call(bf16[616,512]{1,0:T(8,128)(2,1)} %bitcast.6, s32[1,512]{1,0:T(1,128)} %bitcast.7, s32[1,512]{1,0:T(1,128)} %bitcast.8, bf16[616,512]{1,0:T(8,128)(2,1)} %w_in_in.1, bf16[512,512]{1,0:T(8,128)(2,1)} %w_out_in.1, bf16[512,512]{1,0:T(8,128)(2,1)} %w_point_in.1, ...), custom_call_target="tpu_custom_call" | custom-call | tf_op jit(solution)/shard_map/pallas_call | solution.py:776
  79.2 3.1 %shard_map.120 = (bf16[2048,512]{1,0:T(8,128)(2,1)}, f32[616,512]{1,0:T(8,128)}, f32[512,512]{1,0:T(8,128)}, f32[512,512]{1,0:T(8,128)}, f32[9,512]{1,0:T(8,128)}) custom-call(bf16[2048,512]{1,0:T(8,128)(2,1)S(1)} %get-tuple-element.12.latent_in, bf16[1664,512]{1,0:T(8,128)(2,1)S(1)} %get-tuple-element.13.total), custom_call_target="tpu_custom_call" | custom-call | tf_op jit(solution)/shard_map/pallas_call | solution.py:869
